TPU v7x, 32 devices: a whole 2x2x4 slice. The times are simulated.
32 devices in a mesh: section: 4 (over z), expert: 8 (over y, x, core).
Axes of the slice: x: 2, y: 2, z: 4, core: 2. Of those that a mesh axis runs over, the one named last changes fastest.
Arguments:
- x_saved: bfloat16 [4, 8, 128, 2560], P('section', None, 'expert'), may hold values from -6 to 6
- routes: int32 [4, 8, 128, 2], P('section', None, 'expert'), may hold values from 0 to 3, all different within a row; in each aligned block of 16 rows (0 to 15, 16 to 31, ..., all dimensions but the last counted through in order) at most 12 rows name the same one
- gates: float32 [4, 8, 128, 2], P('section', None, 'expert'), may hold values from 0.1 to 0.6
- cotangent: bfloat16 [8, 128, 2560], P(None, 'expert', 'section'), may hold values from -6 to 6
- w_gate: bfloat16 [4, 3072, 2560], P('section', 'expert'), may hold values from -0.125 to 0.125
- w_up: bfloat16 [4, 3072, 2560], P('section', 'expert'), may hold values from -0.125 to 0.125
- w_down: bfloat16 [4, 3072, 2560], P('section', 'expert'), may hold values from -0.21875 to 0.21875
Outputs:
- grad_inputs: bfloat16 [4, 8, 128, 2560], P('section', None, 'expert')
- grad_gate: bfloat16 [4, 3072, 2560], P('section', 'expert')
- grad_up: bfloat16 [4, 3072, 2560], P('section', 'expert')
- grad_down: bfloat16 [4, 3072, 2560], P('section', 'expert')
Inputs may be any that keep to these rules, and one draw needn't show every extreme that they name: `routes`: each token names 2 different experts. In each aligned block of 16 tokens (one device's tokens of one section and micro-batch), no expert is named by more than 12 tokens, and in some blocks one is named by exactly 12.
All inputs are finite; a program needn't handle non-finite values.
Results may differ from a plain program's by a relative error of at most 0.025.
Values may be sent and summed in bfloat16 or wider, within the bound.
A program may use at most 128 MiB of HBM per device.

v0:
```python
from functools import partial

import jax
import jax.numpy as jnp
from jax import lax
from jax.sharding import PartitionSpec as P

SPLIT = 2


CONTRACT_ROWS = (((0,), (0,)), ((), ()))
CONTRACT_COLS = (((1,), (1,)), ((), ()))


def passed_along(value, axis, steps):
    count = lax.axis_size(axis)
    first, last = (max(0, -steps), min(count, count - steps))
    return lax.ppermute(value, axis, [(source, source + steps) for source in range(first, last)])


def swish_parts(pre_gate):
    sigmoid = jax.nn.sigmoid(pre_gate)
    return (pre_gate * sigmoid, sigmoid * (1.0 + pre_gate * (1.0 - sigmoid)))


def slot_index(route_rows, experts, capacity):
    route_hot = (route_rows[:, None] == jnp.arange(experts, dtype=jnp.int32)[None, :]).astype(
        jnp.int32
    )
    earlier = jnp.cumsum(route_hot, axis=0) - route_hot
    return route_rows * capacity + jnp.sum(earlier * route_hot, axis=1)


def spread(slot_rows, experts, capacity):
    leading = slot_rows.shape[:-2]
    features = slot_rows.shape[-1]
    shaped = slot_rows.reshape(leading + (experts, 1, capacity, features))
    widened = jnp.broadcast_to(shaped, leading + (experts, SPLIT, capacity, features))
    return widened.reshape(leading + (experts * SPLIT, capacity, features))


def forward_parts(rows_in, gate_rows, up_rows):
    pre_gate = lax.dot_general(
        rows_in, gate_rows, CONTRACT_COLS, preferred_element_type=jnp.float32
    )
    pre_up = lax.dot_general(rows_in, up_rows, CONTRACT_COLS, preferred_element_type=jnp.float32)
    return (pre_gate, pre_up)


def backward_rows(rows_grad, pre_gate, pre_up, gate_rows, up_rows, down_rows):
    swished, slope_act = swish_parts(pre_gate)
    hidden_act = (swished * pre_up).astype(jnp.bfloat16)
    d_hidden = lax.dot_general(
        rows_grad, down_rows, CONTRACT_COLS, preferred_element_type=jnp.float32
    )
    d_gate = (d_hidden * pre_up * slope_act).astype(jnp.bfloat16)
    d_up = (d_hidden * swished).astype(jnp.bfloat16)
    slice_part = jnp.dot(d_gate, gate_rows, preferred_element_type=jnp.float32)
    slice_part = slice_part + jnp.dot(d_up, up_rows, preferred_element_type=jnp.float32)
    return (slice_part.astype(jnp.bfloat16), hidden_act, d_gate, d_up)


def weight_terms(rows_in, rows_grad, hidden_act, d_gate, d_up):
    return (
        lax.dot_general(d_gate, rows_in, CONTRACT_ROWS, preferred_element_type=jnp.float32),
        lax.dot_general(d_up, rows_in, CONTRACT_ROWS, preferred_element_type=jnp.float32),
        lax.dot_general(hidden_act, rows_grad, CONTRACT_ROWS, preferred_element_type=jnp.float32),
    )


def on_device(x_saved, routes, gates, cotangent, w_gate, w_up, w_down):
    sections = lax.axis_size("section")
    devices_wide = lax.axis_size("expert")
    section_index = lax.axis_index("section")
    experts = devices_wide // SPLIT
    batches = x_saved.shape[1]
    tokens_dev = x_saved.shape[2]
    model_width = x_saved.shape[3]
    top_count = routes.shape[3]
    capacity = max(2, 3 * tokens_dev * top_count // (2 * experts))
    slot_count = experts * capacity
    rows_total = devices_wide * capacity
    gate_rows = w_gate[0]
    up_rows = w_up[0]
    down_rows = w_down[0]
    hidden_dev = gate_rows.shape[0]
    route_flat = routes[0].reshape(batches, tokens_dev * top_count)
    slot_table = jax.vmap(partial(slot_index, experts=experts, capacity=capacity))(route_flat)
    placing = (
        jnp.arange(slot_count, dtype=jnp.int32)[None, :, None] == slot_table[:, None, :]
    ).astype(jnp.bfloat16)
    input_repeat = jnp.repeat(x_saved[0], top_count, axis=1)
    input_slots = jnp.einsum(
        "bsr,brd->bsd", placing, input_repeat, preferred_element_type=jnp.float32
    ).astype(jnp.bfloat16)
    top_grads = lax.all_gather(cotangent, "section", axis=2, tiled=True)
    saved_state = tuple((jnp.zeros((hidden_dev, model_width), jnp.float32) for unused in range(3)))

    def clock_tick(tick_index, carried):
        arriving, results, saved_state = carried
        micro_batch = tick_index - (sections - 1 - section_index)
        active = jnp.logical_and(micro_batch >= 0, micro_batch < batches)
        chosen = jnp.clip(micro_batch, 0, batches - 1)
        upstream = jnp.where(section_index == sections - 1, top_grads[chosen], arriving)
        scaled = jnp.repeat(upstream, top_count, axis=0).astype(jnp.float32) * gates[
            0, chosen
        ].reshape(-1, 1)
        grad_slots = jnp.dot(
            placing[chosen], scaled.astype(jnp.bfloat16), preferred_element_type=jnp.float32
        ).astype(jnp.bfloat16)
        rows_in, rows_grad = (
            lax.all_to_all(
                spread(input_slots[chosen], experts, capacity),
                "expert",
                split_axis=0,
                concat_axis=0,
                tiled=True,
            ),
            lax.all_to_all(
                spread(grad_slots, experts, capacity),
                "expert",
                split_axis=0,
                concat_axis=0,
                tiled=True,
            ),
        )
        rows_in = rows_in.reshape(rows_total, model_width)
        rows_grad = rows_grad.reshape(rows_total, model_width)

        def section_work(saved_state):
            pre_gate, pre_up = forward_parts(rows_in, gate_rows, up_rows)
            slice_part, hidden_act, d_gate, d_up = backward_rows(
                rows_grad, pre_gate, pre_up, gate_rows, up_rows, down_rows
            )
            saved_state = jax.tree.map(
                jnp.add, saved_state, weight_terms(rows_in, rows_grad, hidden_act, d_gate, d_up)
            )
            return (slice_part, saved_state)

        def skipped(saved_state):
            return (jnp.zeros((rows_total, model_width), jnp.bfloat16), saved_state)

        slice_part, saved_state = lax.cond(active, section_work, skipped, saved_state)
        returned = lax.all_to_all(
            slice_part.reshape(devices_wide, capacity, model_width),
            "expert",
            split_axis=0,
            concat_axis=0,
            tiled=True,
        )
        summed = jnp.sum(
            returned.reshape(experts, SPLIT, capacity, model_width).astype(jnp.float32), axis=1
        )
        picked = jnp.take(summed.reshape(slot_count, model_width), slot_table[chosen], axis=0)
        outgoing = (
            upstream.astype(jnp.float32)
            + jnp.sum(picked.reshape(tokens_dev, top_count, model_width), axis=1)
        ).astype(jnp.bfloat16)
        written = jnp.where(active, outgoing, results[chosen])
        results = lax.dynamic_update_index_in_dim(results, written, chosen, 0)
        arriving = passed_along(outgoing, "section", -1)
        return (arriving, results, saved_state)

    initial = (
        jnp.zeros((tokens_dev, model_width), jnp.bfloat16),
        jnp.zeros((batches, tokens_dev, model_width), jnp.bfloat16),
        saved_state,
    )
    arriving, results, saved_state = lax.fori_loop(0, sections + batches - 1, clock_tick, initial)
    grad_gate, grad_up, grad_down = [
        (running_sum / batches).astype(jnp.bfloat16)[None] for running_sum in saved_state
    ]
    return (results[None], grad_gate, grad_up, grad_down)


def solution(mesh):
    in_specs = (
        P("section", None, "expert", None),
        P("section", None, "expert", None),
        P("section", None, "expert", None),
        P(None, "expert", "section"),
        P("section", "expert", None),
        P("section", "expert", None),
        P("section", "expert", None),
    )
    out_specs = (
        P("section", None, "expert", None),
        P("section", "expert", None),
        P("section", "expert", None),
        P("section", "expert", None),
    )
    return jax.shard_map(
        on_device, mesh=mesh, in_specs=in_specs, out_specs=out_specs, check_vma=False
    )
```

profile of v0, /device:TPU:0, one launch (start us, length us, event | category | flops | bytes accessed | tf_op | source)
XLA Modules:
  0.0 894.8 jit_solution(7123500940123865587)
XLA Ops:
  7.3 19.4 %all_gather.3 = bf16[8,16,2560]{2,1,0:T(8,128)(2,1)} all-gather(bf16[8,16,640]{2,1,0:T(8,128)(2,1)S(1)} %copy-done.10), channel_id=1, replica_groups=mesh['section'=4,'expert'=8] {'section'}, dimensions={2}, use_global_device_ids=true | all-gather | bytes 819200 | tf_op jit(solution)/shard_map/all_gather | solution.py:96
  34.8 852.2 %while.23 = (s32[]{:T(128)}, bf16[16,2560]{1,0:T(8,128)(2,1)S(1)}, bf16[8,16,2560]{2,1,0:T(8,128)(2,1)}, f32[384,2560]{1,0:T(8,128)}, f32[384,2560]{1,0:T(8,128)...) while((s32[]{:T(128)}, bf16[16,2560]{1,0:T(8,128)(2,1)S(1)}, ...), condition=%wide.region_7.8_spmd, body=%wide.region_2.7_spmd.sunk | while | flops 1522939136 | bytes 161909296 | solution.py:169
  58.1 10.9 %all-to-all-done.1 = bf16[8,12,2560]{2,1,0:T(8,128)(2,1)S(1)} async-done(((bf16[8,12,2560]{2,1,0:T(8,128)(2,1)}), bf16[8,12,2560]{2,1,0:T(8,128)(2,1)S(1)}, u32[]{:S(2)}, u32[]{:S(2)}) %all-to-all-start.1) | async-done | bytes 491552 | tf_op jit(solution)/shard_map/while/body/eval_jaxpr/all_to_all | solution.py:112
  118.0 10.9 %all-to-all-done.1 = bf16[8,12,2560]{2,1,0:T(8,128)(2,1)S(1)} async-done(((bf16[8,12,2560]{2,1,0:T(8,128)(2,1)}), bf16[8,12,2560]{2,1,0:T(8,128)(2,1)S(1)}, u32[]{:S(2)}, u32[]{:S(2)}) %all-to-all-start.1) | async-done | bytes 491552 | tf_op jit(solution)/shard_map/while/body/eval_jaxpr/all_to_all | solution.py:112
  177.9 10.9 %all-to-all-done.1 = bf16[8,12,2560]{2,1,0:T(8,128)(2,1)S(1)} async-done(((bf16[8,12,2560]{2,1,0:T(8,128)(2,1)}), bf16[8,12,2560]{2,1,0:T(8,128)(2,1)S(1)}, u32[]{:S(2)}, u32[]{:S(2)}) %all-to-all-start.1) | async-done | bytes 491552 | tf_op jit(solution)/shard_map/while/body/eval_jaxpr/all_to_all | solution.py:112
  196.1 10.2 %all-to-all-done.2 = bf16[8,12,2560]{2,1,0:T(8,128)(2,1)S(1)} async-done(((bf16[8,12,2560]{2,1,0:T(8,128)(2,1)}), bf16[8,12,2560]{2,1,0:T(8,128)(2,1)S(1)}, u32[]{:S(2)}, u32[]{:S(2)}) %all-to-all-start.2) | async-done | bytes 491552 | tf_op jit(solution)/shard_map/while/body/eval_jaxpr/all_to_all | solution.py:144
  209.8 56.1 %collective-permute-done = bf16[16,2560]{1,0:T(8,128)(2,1)S(1)} collective-permute-done((bf16[16,2560]{1,0:T(8,128)(2,1)S(1)}, bf16[16,2560]{1,0:T(8,128)(2,1)S(1)}, u32[]{:S(2)}, u32[]{:S(2)}) %collective-permute-start) | collective-permute-done | bytes 81952 | tf_op jit(solution)/shard_map/while/body/eval_jaxpr/ppermute | solution.py:18
  288.9 10.9 %all-to-all-done.1 = bf16[8,12,2560]{2,1,0:T(8,128)(2,1)S(1)} async-done(((bf16[8,12,2560]{2,1,0:T(8,128)(2,1)}), bf16[8,12,2560]{2,1,0:T(8,128)(2,1)S(1)}, u32[]{:S(2)}, u32[]{:S(2)}) %all-to-all-start.1) | async-done | bytes 491552 | tf_op jit(solution)/shard_map/while/body/eval_jaxpr/all_to_all | solution.py:112
  299.8 18.5 %conditional.2 = (bf16[96,2560]{1,0:T(8,128)(2,1)}, f32[384,2560]{1,0:T(8,128)}, f32[384,2560]{1,0:T(8,128)}, f32[384,2560]{1,0:T(8,128)}) conditional(s32[]{:T(128)} %convert_element_type.144, (f32[384,2560]{1,0:T(8,128)}, f32[384,2560]{1,0:T(8,128)}, f32[384,2560]{1,0:T(8,128)}) %tuple.55, (bf16[8,12,2560]{2,1,0:T(8,128)(2,1)S(1)}, ...), branch_computations={%region_3.3_spmd, %region_4.4_spmd} | conditional | flops 1514090496 | bytes 146325760 | solution.py:143
  366.6 10.9 %all-to-all-done.1 = bf16[8,12,2560]{2,1,0:T(8,128)(2,1)S(1)} async-done(((bf16[8,12,2560]{2,1,0:T(8,128)(2,1)}), bf16[8,12,2560]{2,1,0:T(8,128)(2,1)S(1)}, u32[]{:S(2)}, u32[]{:S(2)}) %all-to-all-start.1) | async-done | bytes 491552 | tf_op jit(solution)/shard_map/while/body/eval_jaxpr/all_to_all | solution.py:112
  377.5 18.5 %conditional.2 = (bf16[96,2560]{1,0:T(8,128)(2,1)}, f32[384,2560]{1,0:T(8,128)}, f32[384,2560]{1,0:T(8,128)}, f32[384,2560]{1,0:T(8,128)}) conditional(s32[]{:T(128)} %convert_element_type.144, (f32[384,2560]{1,0:T(8,128)}, f32[384,2560]{1,0:T(8,128)}, f32[384,2560]{1,0:T(8,128)}) %tuple.55, (bf16[8,12,2560]{2,1,0:T(8,128)(2,1)S(1)}, ...), branch_computations={%region_3.3_spmd, %region_4.4_spmd} | conditional | flops 1514090496 | bytes 146325760 | solution.py:143
  444.2 10.9 %all-to-all-done.1 = bf16[8,12,2560]{2,1,0:T(8,128)(2,1)S(1)} async-done(((bf16[8,12,2560]{2,1,0:T(8,128)(2,1)}), bf16[8,12,2560]{2,1,0:T(8,128)(2,1)S(1)}, u32[]{:S(2)}, u32[]{:S(2)}) %all-to-all-start.1) | async-done | bytes 491552 | tf_op jit(solution)/shard_map/while/body/eval_jaxpr/all_to_all | solution.py:112
  455.1 18.5 %conditional.2 = (bf16[96,2560]{1,0:T(8,128)(2,1)}, f32[384,2560]{1,0:T(8,128)}, f32[384,2560]{1,0:T(8,128)}, f32[384,2560]{1,0:T(8,128)}) conditional(s32[]{:T(128)} %convert_element_type.144, (f32[384,2560]{1,0:T(8,128)}, f32[384,2560]{1,0:T(8,128)}, f32[384,2560]{1,0:T(8,128)}) %tuple.55, (bf16[8,12,2560]{2,1,0:T(8,128)(2,1)S(1)}, ...), branch_computations={%region_3.3_spmd, %region_4.4_spmd} | conditional | flops 1514090496 | bytes 146325760 | solution.py:143
  521.8 10.9 %all-to-all-done.1 = bf16[8,12,2560]{2,1,0:T(8,128)(2,1)S(1)} async-done(((bf16[8,12,2560]{2,1,0:T(8,128)(2,1)}), bf16[8,12,2560]{2,1,0:T(8,128)(2,1)S(1)}, u32[]{:S(2)}, u32[]{:S(2)}) %all-to-all-start.1) | async-done | bytes 491552 | tf_op jit(solution)/shard_map/while/body/eval_jaxpr/all_to_all | solution.py:112
  532.8 18.5 %conditional.2 = (bf16[96,2560]{1,0:T(8,128)(2,1)}, f32[384,2560]{1,0:T(8,128)}, f32[384,2560]{1,0:T(8,128)}, f32[384,2560]{1,0:T(8,128)}) conditional(s32[]{:T(128)} %convert_element_type.144, (f32[384,2560]{1,0:T(8,128)}, f32[384,2560]{1,0:T(8,128)}, f32[384,2560]{1,0:T(8,128)}) %tuple.55, (bf16[8,12,2560]{2,1,0:T(8,128)(2,1)S(1)}, ...), branch_computations={%region_3.3_spmd, %region_4.4_spmd} | conditional | flops 1514090496 | bytes 146325760 | solution.py:143
  599.5 10.9 %all-to-all-done.1 = bf16[8,12,2560]{2,1,0:T(8,128)(2,1)S(1)} async-done(((bf16[8,12,2560]{2,1,0:T(8,128)(2,1)}), bf16[8,12,2560]{2,1,0:T(8,128)(2,1)S(1)}, u32[]{:S(2)}, u32[]{:S(2)}) %all-to-all-start.1) | async-done | bytes 491552 | tf_op jit(solution)/shard_map/while/body/eval_jaxpr/all_to_all | solution.py:112
  610.4 18.5 %conditional.2 = (bf16[96,2560]{1,0:T(8,128)(2,1)}, f32[384,2560]{1,0:T(8,128)}, f32[384,2560]{1,0:T(8,128)}, f32[384,2560]{1,0:T(8,128)}) conditional(s32[]{:T(128)} %convert_element_type.144, (f32[384,2560]{1,0:T(8,128)}, f32[384,2560]{1,0:T(8,128)}, f32[384,2560]{1,0:T(8,128)}) %tuple.55, (bf16[8,12,2560]{2,1,0:T(8,128)(2,1)S(1)}, ...), branch_computations={%region_3.3_spmd, %region_4.4_spmd} | conditional | flops 1514090496 | bytes 146325760 | solution.py:143
  677.1 10.9 %all-to-all-done.1 = bf16[8,12,2560]{2,1,0:T(8,128)(2,1)S(1)} async-done(((bf16[8,12,2560]{2,1,0:T(8,128)(2,1)}), bf16[8,12,2560]{2,1,0:T(8,128)(2,1)S(1)}, u32[]{:S(2)}, u32[]{:S(2)}) %all-to-all-start.1) | async-done | bytes 491552 | tf_op jit(solution)/shard_map/while/body/eval_jaxpr/all_to_all | solution.py:112
  688.0 18.5 %conditional.2 = (bf16[96,2560]{1,0:T(8,128)(2,1)}, f32[384,2560]{1,0:T(8,128)}, f32[384,2560]{1,0:T(8,128)}, f32[384,2560]{1,0:T(8,128)}) conditional(s32[]{:T(128)} %convert_element_type.144, (f32[384,2560]{1,0:T(8,128)}, f32[384,2560]{1,0:T(8,128)}, f32[384,2560]{1,0:T(8,128)}) %tuple.55, (bf16[8,12,2560]{2,1,0:T(8,128)(2,1)S(1)}, ...), branch_computations={%region_3.3_spmd, %region_4.4_spmd} | conditional | flops 1514090496 | bytes 146325760 | solution.py:143
  754.7 10.9 %all-to-all-done.1 = bf16[8,12,2560]{2,1,0:T(8,128)(2,1)S(1)} async-done(((bf16[8,12,2560]{2,1,0:T(8,128)(2,1)}), bf16[8,12,2560]{2,1,0:T(8,128)(2,1)S(1)}, u32[]{:S(2)}, u32[]{:S(2)}) %all-to-all-start.1) | async-done | bytes 491552 | tf_op jit(solution)/shard_map/while/body/eval_jaxpr/all_to_all | solution.py:112
  765.6 18.5 %conditional.2 = (bf16[96,2560]{1,0:T(8,128)(2,1)}, f32[384,2560]{1,0:T(8,128)}, f32[384,2560]{1,0:T(8,128)}, f32[384,2560]{1,0:T(8,128)}) conditional(s32[]{:T(128)} %convert_element_type.144, (f32[384,2560]{1,0:T(8,128)}, f32[384,2560]{1,0:T(8,128)}, f32[384,2560]{1,0:T(8,128)}) %tuple.55, (bf16[8,12,2560]{2,1,0:T(8,128)(2,1)S(1)}, ...), branch_computations={%region_3.3_spmd, %region_4.4_spmd} | conditional | flops 1514090496 | bytes 146325760 | solution.py:143
  790.6 10.2 %all-to-all-done.2 = bf16[8,12,2560]{2,1,0:T(8,128)(2,1)S(1)} async-done(((bf16[8,12,2560]{2,1,0:T(8,128)(2,1)}), bf16[8,12,2560]{2,1,0:T(8,128)(2,1)S(1)}, u32[]{:S(2)}, u32[]{:S(2)}) %all-to-all-start.2) | async-done | bytes 491552 | tf_op jit(solution)/shard_map/while/body/eval_jaxpr/all_to_all | solution.py:144
  832.4 10.9 %all-to-all-done.1 = bf16[8,12,2560]{2,1,0:T(8,128)(2,1)S(1)} async-done(((bf16[8,12,2560]{2,1,0:T(8,128)(2,1)}), bf16[8,12,2560]{2,1,0:T(8,128)(2,1)S(1)}, u32[]{:S(2)}, u32[]{:S(2)}) %all-to-all-start.1) | async-done | bytes 491552 | tf_op jit(solution)/shard_map/while/body/eval_jaxpr/all_to_all | solution.py:112
  843.3 18.5 %conditional.2 = (bf16[96,2560]{1,0:T(8,128)(2,1)}, f32[384,2560]{1,0:T(8,128)}, f32[384,2560]{1,0:T(8,128)}, f32[384,2560]{1,0:T(8,128)}) conditional(s32[]{:T(128)} %convert_element_type.144, (f32[384,2560]{1,0:T(8,128)}, f32[384,2560]{1,0:T(8,128)}, f32[384,2560]{1,0:T(8,128)}) %tuple.55, (bf16[8,12,2560]{2,1,0:T(8,128)(2,1)S(1)}, ...), branch_computations={%region_3.3_spmd, %region_4.4_spmd} | conditional | flops 1514090496 | bytes 146325760 | solution.py:143
  (573 shorter events, 677.8 us)
Async XLA Ops:
  38.6 14.9 %all-to-all-start = ((bf16[8,12,2560]{2,1,0:T(8,128)(2,1)}), bf16[8,12,2560]{2,1,0:T(8,128)(2,1)S(1)}, u32[]{:S(2)}, u32[]{:S(2)}) async-start(bf16[8,12,2560]{2,1,0:T(8,128)(2,1)} %bitcast.73), calls=%async_computation | async-start | bytes 1310720 | tf_op jit(solution)/shard_map/while/body/eval_jaxpr/all_to_all | solution.py:119
  54.4 14.6 %all-to-all-start.1 = ((bf16[8,12,2560]{2,1,0:T(8,128)(2,1)}), bf16[8,12,2560]{2,1,0:T(8,128)(2,1)S(1)}, u32[]{:S(2)}, u32[]{:S(2)}) async-start(bf16[8,12,2560]{2,1,0:T(8,128)(2,1)} %bitcast.77), calls=%async_computation.1 | async-start | bytes 1310720 | tf_op jit(solution)/shard_map/while/body/eval_jaxpr/all_to_all | solution.py:112
  71.8 14.6 %all-to-all-start.2 = ((bf16[8,12,2560]{2,1,0:T(8,128)(2,1)}), bf16[8,12,2560]{2,1,0:T(8,128)(2,1)S(1)}, u32[]{:S(2)}, u32[]{:S(2)}) async-start(bf16[8,12,2560]{2,1,0:T(8,128)(2,1)} %reshape.216), calls=%async_computation.2 | async-start | bytes 1310720 | tf_op jit(solution)/shard_map/while/body/eval_jaxpr/all_to_all | solution.py:144
  114.3 14.6 %all-to-all-start.1 = ((bf16[8,12,2560]{2,1,0:T(8,128)(2,1)}), bf16[8,12,2560]{2,1,0:T(8,128)(2,1)S(1)}, u32[]{:S(2)}, u32[]{:S(2)}) async-start(bf16[8,12,2560]{2,1,0:T(8,128)(2,1)} %bitcast.77), calls=%async_computation.1 | async-start | bytes 1310720 | tf_op jit(solution)/shard_map/while/body/eval_jaxpr/all_to_all | solution.py:112
  131.7 14.6 %all-to-all-start.2 = ((bf16[8,12,2560]{2,1,0:T(8,128)(2,1)}), bf16[8,12,2560]{2,1,0:T(8,128)(2,1)S(1)}, u32[]{:S(2)}, u32[]{:S(2)}) async-start(bf16[8,12,2560]{2,1,0:T(8,128)(2,1)} %reshape.216), calls=%async_computation.2 | async-start | bytes 1310720 | tf_op jit(solution)/shard_map/while/body/eval_jaxpr/all_to_all | solution.py:144
  158.7 14.6 %all-to-all-start = ((bf16[8,12,2560]{2,1,0:T(8,128)(2,1)}), bf16[8,12,2560]{2,1,0:T(8,128)(2,1)S(1)}, u32[]{:S(2)}, u32[]{:S(2)}) async-start(bf16[8,12,2560]{2,1,0:T(8,128)(2,1)} %bitcast.73), calls=%async_computation | async-start | bytes 1310720 | tf_op jit(solution)/shard_map/while/body/eval_jaxpr/all_to_all | solution.py:119
  174.2 14.6 %all-to-all-start.1 = ((bf16[8,12,2560]{2,1,0:T(8,128)(2,1)}), bf16[8,12,2560]{2,1,0:T(8,128)(2,1)S(1)}, u32[]{:S(2)}, u32[]{:S(2)}) async-start(bf16[8,12,2560]{2,1,0:T(8,128)(2,1)} %bitcast.77), calls=%async_computation.1 | async-start | bytes 1310720 | tf_op jit(solution)/shard_map/while/body/eval_jaxpr/all_to_all | solution.py:112
  191.6 14.6 %all-to-all-start.2 = ((bf16[8,12,2560]{2,1,0:T(8,128)(2,1)}), bf16[8,12,2560]{2,1,0:T(8,128)(2,1)S(1)}, u32[]{:S(2)}, u32[]{:S(2)}) async-start(bf16[8,12,2560]{2,1,0:T(8,128)(2,1)} %reshape.216), calls=%async_computation.2 | async-start | bytes 1310720 | tf_op jit(solution)/shard_map/while/body/eval_jaxpr/all_to_all | solution.py:144
  208.5 57.4 %collective-permute-start = (bf16[16,2560]{1,0:T(8,128)(2,1)S(1)}, bf16[16,2560]{1,0:T(8,128)(2,1)S(1)}, u32[]{:S(2)}, u32[]{:S(2)}) collective-permute-start(bf16[16,2560]{1,0:T(8,128)(2,1)S(1)} %get-tuple-element.563), channel_id=1, source_target_pairs={{8,0},{16,8},{24,16},{9,1},{17,9},{25,17},{10,2},{18,10},{26,18},{... | collective-permute-start | bytes 245768 | tf_op jit(solution)/shard_map/while/body/eval_jaxpr/ppermute | solution.py:18
  269.7 14.6 %all-to-all-start = ((bf16[8,12,2560]{2,1,0:T(8,128)(2,1)}), bf16[8,12,2560]{2,1,0:T(8,128)(2,1)S(1)}, u32[]{:S(2)}, u32[]{:S(2)}) async-start(bf16[8,12,2560]{2,1,0:T(8,128)(2,1)} %bitcast.73), calls=%async_computation | async-start | bytes 1310720 | tf_op jit(solution)/shard_map/while/body/eval_jaxpr/all_to_all | solution.py:119
  362.9 14.6 %all-to-all-start.1 = ((bf16[8,12,2560]{2,1,0:T(8,128)(2,1)}), bf16[8,12,2560]{2,1,0:T(8,128)(2,1)S(1)}, u32[]{:S(2)}, u32[]{:S(2)}) async-start(bf16[8,12,2560]{2,1,0:T(8,128)(2,1)} %bitcast.77), calls=%async_computation.1 | async-start | bytes 1310720 | tf_op jit(solution)/shard_map/while/body/eval_jaxpr/all_to_all | solution.py:112
  425.0 14.6 %all-to-all-start = ((bf16[8,12,2560]{2,1,0:T(8,128)(2,1)}), bf16[8,12,2560]{2,1,0:T(8,128)(2,1)S(1)}, u32[]{:S(2)}, u32[]{:S(2)}) async-start(bf16[8,12,2560]{2,1,0:T(8,128)(2,1)} %bitcast.73), calls=%async_computation | async-start | bytes 1310720 | tf_op jit(solution)/shard_map/while/body/eval_jaxpr/all_to_all | solution.py:119
  440.5 14.6 %all-to-all-start.1 = ((bf16[8,12,2560]{2,1,0:T(8,128)(2,1)}), bf16[8,12,2560]{2,1,0:T(8,128)(2,1)S(1)}, u32[]{:S(2)}, u32[]{:S(2)}) async-start(bf16[8,12,2560]{2,1,0:T(8,128)(2,1)} %bitcast.77), calls=%async_computation.1 | async-start | bytes 1310720 | tf_op jit(solution)/shard_map/while/body/eval_jaxpr/all_to_all | solution.py:112
  475.6 14.6 %all-to-all-start.2 = ((bf16[8,12,2560]{2,1,0:T(8,128)(2,1)}), bf16[8,12,2560]{2,1,0:T(8,128)(2,1)S(1)}, u32[]{:S(2)}, u32[]{:S(2)}) async-start(bf16[8,12,2560]{2,1,0:T(8,128)(2,1)} %reshape.216), calls=%async_computation.2 | async-start | bytes 1310720 | tf_op jit(solution)/shard_map/while/body/eval_jaxpr/all_to_all | solution.py:144
  502.6 14.6 %all-to-all-start = ((bf16[8,12,2560]{2,1,0:T(8,128)(2,1)}), bf16[8,12,2560]{2,1,0:T(8,128)(2,1)S(1)}, u32[]{:S(2)}, u32[]{:S(2)}) async-start(bf16[8,12,2560]{2,1,0:T(8,128)(2,1)} %bitcast.73), calls=%async_computation | async-start | bytes 1310720 | tf_op jit(solution)/shard_map/while/body/eval_jaxpr/all_to_all | solution.py:119
  553.2 14.6 %all-to-all-start.2 = ((bf16[8,12,2560]{2,1,0:T(8,128)(2,1)}), bf16[8,12,2560]{2,1,0:T(8,128)(2,1)S(1)}, u32[]{:S(2)}, u32[]{:S(2)}) async-start(bf16[8,12,2560]{2,1,0:T(8,128)(2,1)} %reshape.216), calls=%async_computation.2 | async-start | bytes 1310720 | tf_op jit(solution)/shard_map/while/body/eval_jaxpr/all_to_all | solution.py:144
  580.2 14.6 %all-to-all-start = ((bf16[8,12,2560]{2,1,0:T(8,128)(2,1)}), bf16[8,12,2560]{2,1,0:T(8,128)(2,1)S(1)}, u32[]{:S(2)}, u32[]{:S(2)}) async-start(bf16[8,12,2560]{2,1,0:T(8,128)(2,1)} %bitcast.73), calls=%async_computation | async-start | bytes 1310720 | tf_op jit(solution)/shard_map/while/body/eval_jaxpr/all_to_all | solution.py:119
  630.9 14.6 %all-to-all-start.2 = ((bf16[8,12,2560]{2,1,0:T(8,128)(2,1)}), bf16[8,12,2560]{2,1,0:T(8,128)(2,1)S(1)}, u32[]{:S(2)}, u32[]{:S(2)}) async-start(bf16[8,12,2560]{2,1,0:T(8,128)(2,1)} %reshape.216), calls=%async_computation.2 | async-start | bytes 1310720 | tf_op jit(solution)/shard_map/while/body/eval_jaxpr/all_to_all | solution.py:144
  673.4 14.6 %all-to-all-start.1 = ((bf16[8,12,2560]{2,1,0:T(8,128)(2,1)}), bf16[8,12,2560]{2,1,0:T(8,128)(2,1)S(1)}, u32[]{:S(2)}, u32[]{:S(2)}) async-start(bf16[8,12,2560]{2,1,0:T(8,128)(2,1)} %bitcast.77), calls=%async_computation.1 | async-start | bytes 1310720 | tf_op jit(solution)/shard_map/while/body/eval_jaxpr/all_to_all | solution.py:112
  735.5 14.6 %all-to-all-start = ((bf16[8,12,2560]{2,1,0:T(8,128)(2,1)}), bf16[8,12,2560]{2,1,0:T(8,128)(2,1)S(1)}, u32[]{:S(2)}, u32[]{:S(2)}) async-start(bf16[8,12,2560]{2,1,0:T(8,128)(2,1)} %bitcast.73), calls=%async_computation | async-start | bytes 1310720 | tf_op jit(solution)/shard_map/while/body/eval_jaxpr/all_to_all | solution.py:119
  751.0 14.6 %all-to-all-start.1 = ((bf16[8,12,2560]{2,1,0:T(8,128)(2,1)}), bf16[8,12,2560]{2,1,0:T(8,128)(2,1)S(1)}, u32[]{:S(2)}, u32[]{:S(2)}) async-start(bf16[8,12,2560]{2,1,0:T(8,128)(2,1)} %bitcast.77), calls=%async_computation.1 | async-start | bytes 1310720 | tf_op jit(solution)/shard_map/while/body/eval_jaxpr/all_to_all | solution.py:112
  786.1 14.6 %all-to-all-start.2 = ((bf16[8,12,2560]{2,1,0:T(8,128)(2,1)}), bf16[8,12,2560]{2,1,0:T(8,128)(2,1)S(1)}, u32[]{:S(2)}, u32[]{:S(2)}) async-start(bf16[8,12,2560]{2,1,0:T(8,128)(2,1)} %reshape.216), calls=%async_computation.2 | async-start | bytes 1310720 | tf_op jit(solution)/shard_map/while/body/eval_jaxpr/all_to_all | solution.py:144
  813.1 14.6 %all-to-all-start = ((bf16[8,12,2560]{2,1,0:T(8,128)(2,1)}), bf16[8,12,2560]{2,1,0:T(8,128)(2,1)S(1)}, u32[]{:S(2)}, u32[]{:S(2)}) async-start(bf16[8,12,2560]{2,1,0:T(8,128)(2,1)} %bitcast.73), calls=%async_computation | async-start | bytes 1310720 | tf_op jit(solution)/shard_map/while/body/eval_jaxpr/all_to_all | solution.py:119
  863.8 14.6 %all-to-all-start.2 = ((bf16[8,12,2560]{2,1,0:T(8,128)(2,1)}), bf16[8,12,2560]{2,1,0:T(8,128)(2,1)S(1)}, u32[]{:S(2)}, u32[]{:S(2)}) async-start(bf16[8,12,2560]{2,1,0:T(8,128)(2,1)} %reshape.216), calls=%async_computation.2 | async-start | bytes 1310720 | tf_op jit(solution)/shard_map/while/body/eval_jaxpr/all_to_all | solution.py:144
  (87 other events, 379.1 us)
where the time goes:
time: 902 us; the launch traced here: 895 us
  waiting for transfers between devices  449 us (50%)
  local copies, waits for them, and re-layouts  166 us (18%)
  starting transfers between devices  131 us (15%)
  matrix products  90.4 us (10%)
  other arithmetic  35.5 us (4%)
  blocking collectives  19.4 us (2%)
    all_to_all x11, waiting for transfers between devices, clock_tick(): lax.all_to_all(spread(input_slots[chosen], experts, capacity), 'expert',...  120 us
    all_to_all x11, waiting for transfers between devices, clock_tick(): lax.all_to_all(slice_part.reshape(devices_wide, capacity, model_width), '...  112 us
    all_to_all x11, waiting for transfers between devices, clock_tick(): lax.all_to_all(spread(grad_slots, experts, capacity), 'expert', split_axi...  111 us
    ppermute x11, waiting for transfers between devices, passed_along(): lax.ppermute(value, axis, [(source, source + steps) for source in range(f...  107 us
    cond x128, local copies, waits for them, and re-layouts  58.2 us
    all_to_all x11, starting transfers between devices, clock_tick(): lax.all_to_all(spread(grad_slots, experts, capacity), 'expert', split_axi...  39.1 us
    all_to_all x11, starting transfers between devices, clock_tick(): lax.all_to_all(slice_part.reshape(devices_wide, capacity, model_width), '...  39 us
    all_to_all x11, starting transfers between devices, clock_tick(): lax.all_to_all(spread(input_slots[chosen], experts, capacity), 'expert',...  39 us
  transfers between devices with their start and end apart: 44, of which 44 were waited for; matrix products, arithmetic and copies ran while one was open for 3% of the time, Pallas kernels for 0%

commit v1 on v0

v1 whole, which is shorter than its diff:
```python
import functools

import jax
import jax.numpy as jnp
from jax import lax
from jax.experimental import pallas as pl
from jax.experimental.pallas import tpu as pltpu
from jax.sharding import PartitionSpec as P

SPLIT = 2
MESH = pl.DeviceIdType.MESH
COLS = (((1,), (1,)), ((), ()))
F32 = jnp.float32
BF16 = jnp.bfloat16


def relay_kernel(
    sections, experts, batches, groups, blk, tile,
    x_ref, cot_ref, gates_ref, place_ref, place_x_ref, place_t_ref, wg_ref, wu_ref, wd_ref,
    out_ref, dwg_ref, dwu_ref, dwd_ref,
    up_buf, x_send, x_rows, g_send, g_rows, r_send, r_recv, w_other, acts, acts_send, acts_t,
    slope_buf, swish_buf,
    x_ss, x_rs, g_ss, g_rs, r_ss, r_rs, hop_ss, hop_rs, top_ss, top_rs, w_ss, w_rs,
    px_ss, px_rs, pg_ss, pg_rs, pa_ss, pa_rs,
):
    section = lax.axis_index("section")
    place_in = lax.axis_index("expert")
    chip = place_in // SPLIT
    core = place_in % SPLIT
    other = chip * SPLIT + (1 - core)
    last = section == sections - 1
    rows = experts * blk
    width = x_ref.shape[2]
    hidden = wg_ref.shape[0]
    piece = cot_ref.shape[2]
    gathered = piece == width

    def remote(src, dst, ss, rs, sec, exp):
        return pltpu.make_async_remote_copy(
            src_ref=src, dst_ref=dst, send_sem=ss, recv_sem=rs,
            device_id=(sec, exp), device_id_type=MESH,
        )

    def peer(step):
        return lax.rem(chip + step, experts)

    barrier = pltpu.get_barrier_semaphore()
    for step in range(1, experts):
        pl.semaphore_signal(
            barrier, inc=1, device_id=(section, peer(step) * SPLIT + core), device_id_type=MESH
        )
    pl.semaphore_signal(barrier, inc=1, device_id=(section, other), device_id_type=MESH)
    for step in range(1, sections):
        pl.semaphore_signal(
            barrier, inc=1, device_id=(lax.rem(section + step, sections), place_in),
            device_id_type=MESH,
        )
    pl.semaphore_wait(barrier, experts - 1 + 1 + sections - 1)

    def exchange(send, recv, ss, rs, g, step):
        to = peer(step)
        return remote(
            send.at[g, to], recv.at[g, chip], ss.at[g, to], rs.at[g, chip],
            section, to * SPLIT + core,
        )

    def arrival(send, recv, ss, rs, g, step):
        source = peer(step)
        return remote(
            send.at[g, source], recv.at[g, source], ss.at[g, source], rs.at[g, source],
            section, source * SPLIT + core,
        )

    def send_all(send, recv, ss, rs, g):
        for step in range(1, experts):
            exchange(send, recv, ss, rs, g, step).start()

    def wait_all(send, recv, ss, rs, g):
        for step in range(1, experts):
            arrival(send, recv, ss, rs, g, step).wait_recv()

    def wait_sent(send, recv, ss, rs, g):
        for step in range(1, experts):
            exchange(send, recv, ss, rs, g, step).wait_send()

    def top_copy(g):
        return remote(
            cot_ref.at[g], up_buf.at[g, :, pl.ds(pl.multiple_of(section * piece, 128), piece)],
            top_ss.at[g], top_rs.at[g, section], sections - 1, place_in,
        )

    def hop_copy(g):
        return remote(
            out_ref.at[g], up_buf.at[g], hop_ss.at[g], hop_rs.at[g],
            jnp.maximum(section - 1, 0), place_in,
        )

    def to_partner(buf, ss, rs, g):
        return remote(buf.at[0, g], buf.at[1, g], ss.at[g], rs.at[g], section, other)

    def acts_copy(g):
        return remote(
            acts_send.at[g], acts.at[1, g], pa_ss.at[g], pa_rs.at[g], section, other
        )

    own_w = (wg_ref, wu_ref, wd_ref)
    weight_copies = [
        remote(own_w[i], w_other.at[i], w_ss.at[i], w_rs.at[i], section, other) for i in range(3)
    ]

    @pl.loop(0, groups)
    def _(g):
        if not gathered:
            @pl.when(jnp.logical_not(last))
            def _():
                top_copy(g).start()

        placed = jnp.dot(place_x_ref[g], x_ref[g], preferred_element_type=F32).astype(BF16)
        x_send[g] = placed.reshape(experts, blk, width)
        send_all(x_send, x_rows.at[0], x_ss, x_rs, g)
        x_rows[0, g, chip] = x_send[g, chip]

    for copy in weight_copies:
        copy.start()
    for copy in weight_copies:
        copy.wait_recv()

    def weights(which, half):
        return own_w[which] if half == 0 else w_other.at[which]

    def forward(g):
        wait_all(x_send, x_rows.at[0], x_ss, x_rs, g)
        to_partner(x_rows, px_ss, px_rs, g).start()
        rows_in = x_rows[0, g].reshape(rows, width)
        slot = lax.rem(g, 2)
        for half in range(2):
            pre_gate = lax.dot_general(
                rows_in, weights(0, half)[...], COLS, preferred_element_type=F32
            )
            pre_up = lax.dot_general(
                rows_in, weights(1, half)[...], COLS, preferred_element_type=F32
            )
            sigmoid = jax.nn.sigmoid(pre_gate)
            swished = pre_gate * sigmoid
            columns = pl.ds(half * hidden, hidden)
            swish_buf[slot, :, columns] = swished
            slope_buf[slot, :, columns] = pre_up * (sigmoid * (1.0 + pre_gate * (1.0 - sigmoid)))
            act = (swished * pre_up).astype(BF16)
            third = pl.ds(2 * hidden, hidden)
            if half == 0:
                acts[0, g, :, third] = act
            else:
                acts_send[g, :, third] = act

    forward(0)

    @pl.loop(0, groups)
    def _(g):
        @pl.when(last)
        def _():
            if gathered:
                up_buf[g] = cot_ref[g]
            else:
                for z in range(sections - 1):
                    remote(
                        cot_ref.at[g], up_buf.at[g, :, pl.ds(z * piece, piece)],
                        top_ss.at[g], top_rs.at[g, z], section, place_in,
                    ).wait_recv()
                up_buf[g, :, pl.ds((sections - 1) * piece, piece)] = cot_ref[g]

        @pl.when(jnp.logical_not(last))
        def _():
            hop_copy(g).wait_recv()

        upstream = up_buf[g].astype(F32)
        scaled = jnp.concatenate(
            [(upstream * gates_ref[g, k]).astype(BF16) for k in range(gates_ref.shape[1])], axis=0
        )
        placed = jnp.dot(place_ref[g], scaled, preferred_element_type=F32).astype(BF16)
        g_send[g] = placed.reshape(experts, blk, width)
        send_all(g_send, g_rows.at[0], g_ss, g_rs, g)
        g_rows[0, g, chip] = g_send[g, chip]

        @pl.when(g + 1 < groups)
        def _():
            forward(g + 1)

        wait_all(g_send, g_rows.at[0], g_ss, g_rs, g)
        to_partner(g_rows, pg_ss, pg_rs, g).start()
        rows_grad = g_rows[0, g].reshape(rows, width)
        slot = lax.rem(g, 2)
        slopes = []
        for half in range(2):
            d_hidden = lax.dot_general(
                rows_grad, weights(2, half)[...], COLS, preferred_element_type=F32
            )
            columns = pl.ds(half * hidden, hidden)
            d_gate = (d_hidden * slope_buf[slot, :, columns]).astype(BF16)
            d_up = (d_hidden * swish_buf[slot, :, columns]).astype(BF16)
            slopes.append((d_gate, d_up))
            if half == 0:
                acts[0, g, :, pl.ds(0, hidden)] = d_gate
                acts[0, g, :, pl.ds(hidden, hidden)] = d_up
            else:
                acts_send[g, :, pl.ds(0, hidden)] = d_gate
                acts_send[g, :, pl.ds(hidden, hidden)] = d_up

        @pl.loop(0, width // tile)
        def _(t):
            columns = pl.ds(pl.multiple_of(t * tile, 128), tile)
            total = jnp.zeros((rows, tile), F32)
            for half in range(2):
                for which in range(2):
                    total += jnp.dot(
                        slopes[half][which], weights(which, half)[:, columns],
                        preferred_element_type=F32,
                    )
            r_send[g, :, :, columns] = total.astype(BF16).reshape(experts, blk, tile)

        send_all(r_send, r_recv, r_ss, r_rs, g)
        r_recv[g, chip] = r_send[g, chip]
        acts_copy(g).start()
        wait_all(r_send, r_recv, r_ss, r_rs, g)
        back = jnp.dot(
            place_t_ref[g], r_recv[g].reshape(rows, width), preferred_element_type=F32
        )
        out_ref[g] = (up_buf[g].astype(F32) + back).astype(BF16)

        @pl.when(section > 0)
        def _():
            hop_copy(g).start()

    @pl.loop(0, groups)
    def _(g):
        to_partner(x_rows, px_ss, px_rs, g).wait_recv()
        to_partner(g_rows, pg_ss, pg_rs, g).wait_recv()
        acts_copy(g).wait_recv()

    total_rows = 2 * groups * rows
    for i in range(3):
        acts_t[pl.ds(i * hidden, hidden), :] = (
            acts[:, :, :, pl.ds(i * hidden, hidden)].reshape(total_rows, hidden).T
        )
    share = 1.0 / batches

    @pl.loop(0, width // 256)
    def _(t):
        columns = pl.ds(pl.multiple_of(t * 256, 128), 256)
        rows_in = x_rows[:, :, :, :, columns].reshape(total_rows, 256)
        rows_grad = g_rows[:, :, :, :, columns].reshape(total_rows, 256)
        for i, (result, side) in enumerate(
            ((dwg_ref, rows_in), (dwu_ref, rows_in), (dwd_ref, rows_grad))
        ):
            grad = jnp.dot(
                acts_t[pl.ds(i * hidden, hidden), :], side, preferred_element_type=F32
            )
            result[:, columns] = (grad * share).astype(BF16)

    @pl.loop(0, groups)
    def _(g):
        wait_sent(x_send, x_rows.at[0], x_ss, x_rs, g)
        wait_sent(g_send, g_rows.at[0], g_ss, g_rs, g)
        wait_sent(r_send, r_recv, r_ss, r_rs, g)
        to_partner(x_rows, px_ss, px_rs, g).wait_send()
        to_partner(g_rows, pg_ss, pg_rs, g).wait_send()
        acts_copy(g).wait_send()

        @pl.when(section > 0)
        def _():
            hop_copy(g).wait_send()

        if not gathered:
            @pl.when(jnp.logical_not(last))
            def _():
                top_copy(g).wait_send()

    for copy in weight_copies:
        copy.wait_send()


def on_device(group_rows, x_saved, routes, gates, cotangent, w_gate, w_up, w_down):
    sections = lax.axis_size("section")
    experts = lax.axis_size("expert") // SPLIT
    batches, tokens, width = x_saved.shape[1:]
    top = routes.shape[3]
    hidden = w_gate.shape[1]
    capacity = max(2, 3 * tokens * top // (2 * experts))
    per = 1
    while per * capacity < group_rows and batches % (2 * per) == 0:
        per *= 2
    groups = batches // per
    blk = -(-per * capacity // 16) * 16
    rows = experts * blk
    tile = 512 if width % 512 == 0 else 128

    flat = routes[0].reshape(batches, tokens * top)
    hot = (flat[:, :, None] == jnp.arange(experts, dtype=jnp.int32)).astype(jnp.int32)
    earlier = jnp.cumsum(hot, axis=1) - hot
    within = jnp.sum(earlier * hot, axis=2)
    batch_in = jnp.arange(batches, dtype=jnp.int32)[:, None] % per
    target = (flat * blk + batch_in * capacity + within).reshape(groups, per, tokens, top)
    target = jnp.transpose(target, (0, 3, 1, 2)).reshape(groups, top, per * tokens)
    spots = jnp.arange(rows, dtype=jnp.int32)
    place = (spots[None, :, None] == target.reshape(groups, 1, -1)).astype(BF16)
    place_x = jnp.any(spots[None, :, None, None] == target[:, None], axis=2).astype(BF16)
    place_t = jnp.any(target[:, :, :, None] == spots, axis=1).astype(BF16)
    scales = jnp.transpose(
        gates[0].reshape(groups, per * tokens, top), (0, 2, 1)
    )[..., None]
    x_groups = x_saved[0].reshape(groups, per * tokens, width)
    if cotangent.shape[2] % 128:
        cotangent = lax.all_gather(cotangent, "section", axis=2, tiled=True)
    cot_groups = cotangent.reshape(groups, per * tokens, cotangent.shape[2])

    vmem = pl.BlockSpec(memory_space=pltpu.VMEM)
    slots = (groups, experts, blk, width)
    dma = pltpu.SemaphoreType.DMA
    grad_w = jax.ShapeDtypeStruct((hidden, width), BF16)
    results = pl.pallas_call(
        functools.partial(relay_kernel, sections, experts, batches, groups, blk, tile),
        out_shape=(
            jax.ShapeDtypeStruct((groups, per * tokens, width), BF16), grad_w, grad_w, grad_w,
        ),
        in_specs=[vmem] * 9,
        out_specs=(vmem,) * 4,
        scratch_shapes=[
            pltpu.VMEM((groups, per * tokens, width), BF16),
            pltpu.VMEM(slots, BF16),
            pltpu.VMEM((2,) + slots, BF16),
            pltpu.VMEM(slots, BF16),
            pltpu.VMEM((2,) + slots, BF16),
            pltpu.VMEM(slots, BF16),
            pltpu.VMEM(slots, BF16),
            pltpu.VMEM((3, hidden, width), BF16),
            pltpu.VMEM((2, groups, rows, 3 * hidden), BF16),
            pltpu.VMEM((groups, rows, 3 * hidden), BF16),
            pltpu.VMEM((3 * hidden, 2 * groups * rows), BF16),
            pltpu.VMEM((2, rows, 2 * hidden), F32),
            pltpu.VMEM((2, rows, 2 * hidden), F32),
        ]
        + [dma((groups, experts))] * 6
        + [dma((groups,)), dma((groups,)), dma((groups,)), dma((groups, sections))]
        + [dma((3,))] * 2
        + [dma((groups,))] * 6,
        compiler_params=pltpu.CompilerParams(
            collective_id=0, has_side_effects=True, vmem_limit_bytes=60 * 2**20
        ),
    )(
        x_groups, cot_groups, scales, place, place_x, place_t, w_gate[0], w_up[0], w_down[0]
    )
    grad_inputs = results[0].reshape(1, batches, tokens, width)
    return (grad_inputs, results[1][None], results[2][None], results[3][None])


def solution(mesh):
    rows = P("section", None, "expert", None)
    halves = P("section", "expert", None)
    return jax.shard_map(
        functools.partial(on_device, 12), mesh=mesh,
        in_specs=(rows, rows, rows, P(None, "expert", "section"), halves, halves, halves),
        out_specs=(rows, halves, halves, halves),
        check_vma=False,
    )
```

time: 902 us -> 230 us (0.25)
  waiting for transfers between devices: 449 us -> 0 us
  Pallas kernels: 0 us -> 215 us
  local copies, waits for them, and re-layouts: 166 us -> 11.9 us
  starting transfers between devices: 131 us -> 0 us
  matrix products: 90.4 us -> 0 us
  other arithmetic: 35.5 us -> 2.29 us
  blocking collectives: 19.4 us -> 0 us
    all_to_all x33 -> x0, waiting for transfers between devices: 343 us -> none  [the longest x11 120 us: clock_tick(): lax.all_to_all(spread(input_slots[chosen], experts, capacity), 'expert',...]
    pallas_call x0 -> x1, Pallas kernels: none -> 215 us  [on_device(): pl.pallas_call(functools.partial(relay_kernel, sections, experts, batches...]
    all_to_all x33 -> x0, starting transfers between devices: 117 us -> none  [the longest x11 39.1 us: clock_tick(): lax.all_to_all(spread(grad_slots, experts, capacity), 'expert', split_axi...]
    ppermute x11 -> x0, waiting for transfers between devices: 107 us -> none  [passed_along(): lax.ppermute(value, axis, [(source, source + steps) for source in range(f...]
    dot_general x76 -> x0, matrix products: 90.4 us -> none  [the longest x8 19.4 us: backward_rows(): lax.dot_general(rows_grad, down_rows, CONTRACT_COLS, preferred_element_ty...]
    cond x128 -> x0, local copies, waits for them, and re-layouts: 58.2 us -> none
    reshape x39 -> x0, local copies, waits for them, and re-layouts: 33.4 us -> none  [the longest x11 21.7 us: clock_tick(): slice_part.reshape(devices_wide, capacity, model_width)]
    broadcast_in_dim x47 -> x1, local copies, waits for them, and re-layouts: 23.6 us -> 0.82 us  [on_device(): jnp.transpose(gates[0].reshape(groups, per * tokens, top), (0, 2, 1))]
  transfers between devices with their start and end apart: 44 -> 0, of which waited for: 44 -> 0; matrix products, arithmetic and copies ran while one was open for 3% -> 0% of each run, Pallas kernels for 0% -> 0%
where the time goes in v1:
time: 230 us
  Pallas kernels  215 us (93%)
  local copies, waits for them, and re-layouts  11.9 us (5%)
    pallas_call x1, Pallas kernels, on_device(): pl.pallas_call(functools.partial(relay_kernel, sections, experts, batches...  215 us
    unnamed x10, local copies, waits for them, and re-layouts  10.1 us

profile of v1, /device:TPU:0, one launch (start us, length us, event | category | flops | bytes accessed | tf_op | source)
XLA Modules:
  0.0 229.6 jit_solution(8946521068077315454)
XLA Ops:
  0.6 0.7 copy.41
  1.3 0.8 copy.33
  2.1 0.7 fusion.8
  2.9 0.1 copy.36
  3.0 0.1 copy.35
  3.0 0.1 eq.65
  3.1 0.1 fusion.4
  3.2 0.1 fusion.3
  3.3 0.6 convert_element_type.15.place_t_ref
  4.0 0.8 copy.39.place_x_ref
  4.7 0.8 copy.38.gates_ref
  5.6 0.7 fusion.1.place_ref
  6.3 214.7 %shard_map.102 = (bf16[8,16,2560]{2,1,0:T(8,128)(2,1)}, bf16[384,2560]{1,0:T(8,128)(2,1)}, bf16[384,2560]{1,0:T(8,128)(2,1)}, bf16[384,2560]{1,0:T(8,128)(2,1)}) custom-call(bf16[8,16,2560]{2,1,0:T(8,128)(2,1)} %bitcast.36, bf16[8,16,640]{2,1,0:T(8,128)(2,1)} %cot_ref.1, f32[8,2,16,1]{3,2,1,0:T(8,128)} %copy.38.gates_ref, ...), custom_call_target="tpu_custom_call" | custom-call | tf_op jit(solution)/shard_map/pallas_call | solution.py:319
  221.0 2.0 copy.46
  222.9 0.0 copy-start.1
  222.9 3.1 %copy.47 = bf16[1,384,2560]{2,1,0:T(8,128)(2,1)} copy(bf16[1,384,2560]{2,1,0:T(8,128)(2,1)} %bitcast.35) | data formatting | bytes 3932160
  226.0 0.0 copy-done.1
  226.0 0.0 copy-start
  226.0 1.3 copy.48
  227.3 1.0 copy-done
  228.3 1.3 copy.49
  (2 shorter events, 0.0 us)
Async XLA Ops:
  222.9 3.1 %copy-start.1 = (bf16[384,2560]{1,0:T(8,128)(2,1)S(1)}, bf16[384,2560]{1,0:T(8,128)(2,1)}, u32[]{:S(2)}) copy-start(bf16[384,2560]{1,0:T(8,128)(2,1)} %get-tuple-element.10) | copy-start | bytes 5898244
  226.0 2.3 copy-start

commit v2 on v1

--- a/solution.py
+++ b/solution.py
@@ -108,6 +108,12 @@
         remote(own_w[i], w_other.at[i], w_ss.at[i], w_rs.at[i], section, other) for i in range(3)
     ]
 
+    ahead = jnp.where(last, min(2, groups), groups)
+    early = jnp.minimum(1 + 3 * (sections - 1 - section), groups)
+
+    for copy in weight_copies:
+        copy.start()
+
     @pl.loop(0, groups)
     def _(g):
         if not gathered:
@@ -117,45 +123,46 @@
 
         placed = jnp.dot(place_x_ref[g], x_ref[g], preferred_element_type=F32).astype(BF16)
         x_send[g] = placed.reshape(experts, blk, width)
-        send_all(x_send, x_rows.at[0], x_ss, x_rs, g)
+
+        @pl.when(g < ahead)
+        def _():
+            send_all(x_send, x_rows.at[0], x_ss, x_rs, g)
+
         x_rows[0, g, chip] = x_send[g, chip]
-
-    for copy in weight_copies:
-        copy.start()
-    for copy in weight_copies:
-        copy.wait_recv()
 
     def weights(which, half):
         return own_w[which] if half == 0 else w_other.at[which]
 
-    def forward(g):
+    def forward_half(g, half):
+        rows_in = x_rows[0, g].reshape(rows, width)
+        pre_gate = lax.dot_general(
+            rows_in, weights(0, half)[...], COLS, preferred_element_type=F32
+        )
+        pre_up = lax.dot_general(
+            rows_in, weights(1, half)[...], COLS, preferred_element_type=F32
+        )
+        sigmoid = jax.nn.sigmoid(pre_gate)
+        swished = pre_gate * sigmoid
+        columns = pl.ds(half * hidden, hidden)
+        swish_buf[g, :, columns] = swished
+        slope_buf[g, :, columns] = pre_up * (sigmoid * (1.0 + pre_gate * (1.0 - sigmoid)))
+        act = (swished * pre_up).astype(BF16)
+        third = pl.ds(2 * hidden, hidden)
+        if half == 0:
+            acts[0, g, :, third] = act
+        else:
+            acts_send[g, :, third] = act
+
+    def rows_arrived(g):
         wait_all(x_send, x_rows.at[0], x_ss, x_rs, g)
         to_partner(x_rows, px_ss, px_rs, g).start()
-        rows_in = x_rows[0, g].reshape(rows, width)
-        slot = lax.rem(g, 2)
+
+    def forward(g):
+        rows_arrived(g)
         for half in range(2):
-            pre_gate = lax.dot_general(
-                rows_in, weights(0, half)[...], COLS, preferred_element_type=F32
-            )
-            pre_up = lax.dot_general(
-                rows_in, weights(1, half)[...], COLS, preferred_element_type=F32
-            )
-            sigmoid = jax.nn.sigmoid(pre_gate)
-            swished = pre_gate * sigmoid
-            columns = pl.ds(half * hidden, hidden)
-            swish_buf[slot, :, columns] = swished
-            slope_buf[slot, :, columns] = pre_up * (sigmoid * (1.0 + pre_gate * (1.0 - sigmoid)))
-            act = (swished * pre_up).astype(BF16)
-            third = pl.ds(2 * hidden, hidden)
-            if half == 0:
-                acts[0, g, :, third] = act
-            else:
-                acts_send[g, :, third] = act
-
-    forward(0)
-
-    @pl.loop(0, groups)
-    def _(g):
+            forward_half(g, half)
+
+    def dispatch(g):
         @pl.when(last)
         def _():
             if gathered:
@@ -181,22 +188,17 @@
         send_all(g_send, g_rows.at[0], g_ss, g_rs, g)
         g_rows[0, g, chip] = g_send[g, chip]
 
-        @pl.when(g + 1 < groups)
-        def _():
-            forward(g + 1)
-
+    def backward(g):
         wait_all(g_send, g_rows.at[0], g_ss, g_rs, g)
-        to_partner(g_rows, pg_ss, pg_rs, g).start()
         rows_grad = g_rows[0, g].reshape(rows, width)
-        slot = lax.rem(g, 2)
         slopes = []
         for half in range(2):
             d_hidden = lax.dot_general(
                 rows_grad, weights(2, half)[...], COLS, preferred_element_type=F32
             )
             columns = pl.ds(half * hidden, hidden)
-            d_gate = (d_hidden * slope_buf[slot, :, columns]).astype(BF16)
-            d_up = (d_hidden * swish_buf[slot, :, columns]).astype(BF16)
+            d_gate = (d_hidden * slope_buf[g, :, columns]).astype(BF16)
+            d_up = (d_hidden * swish_buf[g, :, columns]).astype(BF16)
             slopes.append((d_gate, d_up))
             if half == 0:
                 acts[0, g, :, pl.ds(0, hidden)] = d_gate
@@ -219,7 +221,10 @@
 
         send_all(r_send, r_recv, r_ss, r_rs, g)
         r_recv[g, chip] = r_send[g, chip]
+        to_partner(g_rows, pg_ss, pg_rs, g).start()
         acts_copy(g).start()
+
+    def combine(g):
         wait_all(r_send, r_recv, r_ss, r_rs, g)
         back = jnp.dot(
             place_t_ref[g], r_recv[g].reshape(rows, width), preferred_element_type=F32
@@ -229,6 +234,40 @@
         @pl.when(section > 0)
         def _():
             hop_copy(g).start()
+
+    rows_arrived(0)
+    forward_half(0, 0)
+    weight_copies[0].wait_recv()
+    weight_copies[1].wait_recv()
+    forward_half(0, 1)
+
+    @pl.loop(1, early)
+    def _(g):
+        forward(g)
+
+    weight_copies[2].wait_recv()
+
+    @pl.loop(0, groups + 1)
+    def _(g):
+        @pl.when(g < groups)
+        def _():
+            dispatch(g)
+
+        @pl.when(jnp.logical_and(last, g + 2 < groups))
+        def _():
+            send_all(x_send, x_rows.at[0], x_ss, x_rs, g + 2)
+
+        @pl.when(jnp.logical_and(g + 1 >= early, g + 1 < groups))
+        def _():
+            forward(g + 1)
+
+        @pl.when(g > 0)
+        def _():
+            combine(g - 1)
+
+        @pl.when(g < groups)
+        def _():
+            backward(g)
 
     @pl.loop(0, groups)
     def _(g):
@@ -335,8 +374,8 @@
             pltpu.VMEM((2, groups, rows, 3 * hidden), BF16),
             pltpu.VMEM((groups, rows, 3 * hidden), BF16),
             pltpu.VMEM((3 * hidden, 2 * groups * rows), BF16),
-            pltpu.VMEM((2, rows, 2 * hidden), F32),
-            pltpu.VMEM((2, rows, 2 * hidden), F32),
+            pltpu.VMEM((groups, rows, 2 * hidden), F32),
+            pltpu.VMEM((groups, rows, 2 * hidden), F32),
         ]
         + [dma((groups, experts))] * 6
         + [dma((groups,)), dma((groups,)), dma((groups,)), dma((groups, sections))]

time: 230 us -> 202 us (0.88)
  Pallas kernels: 215 us -> 187 us
    pallas_call x1, Pallas kernels: 215 us -> 187 us  [on_device(): pl.pallas_call(functools.partial(relay_kernel, sections, experts, batches...]
where the time goes in v2:
time: 202 us
  Pallas kernels  187 us (93%)
  local copies, waits for them, and re-layouts  11.9 us (6%)
  other arithmetic  2.29 us (1%)
    pallas_call x1, Pallas kernels, on_device(): pl.pallas_call(functools.partial(relay_kernel, sections, experts, batches...  187 us
    unnamed x10, local copies, waits for them, and re-layouts  10.1 us

profile of v2, /device:TPU:0, one launch (start us, length us, event | category | flops | bytes accessed | tf_op | source)
XLA Modules:
  0.0 202.0 jit_solution(12109404991824695758)
XLA Ops:
  0.6 0.7 copy.41
  1.3 0.8 copy.33
  2.1 0.7 fusion.8
  2.9 0.1 copy.36
  3.0 0.1 copy.35
  3.0 0.1 eq.65
  3.1 0.1 fusion.4
  3.2 0.1 fusion.3
  3.3 0.6 convert_element_type.15.place_t_ref
  4.0 0.8 copy.39.place_x_ref
  4.7 0.8 copy.38.gates_ref
  5.6 0.7 fusion.1.place_ref
  6.3 187.2 %shard_map.102 = (bf16[8,16,2560]{2,1,0:T(8,128)(2,1)}, bf16[384,2560]{1,0:T(8,128)(2,1)}, bf16[384,2560]{1,0:T(8,128)(2,1)}, bf16[384,2560]{1,0:T(8,128)(2,1)}) custom-call(bf16[8,16,2560]{2,1,0:T(8,128)(2,1)} %bitcast.36, bf16[8,16,640]{2,1,0:T(8,128)(2,1)} %cot_ref.1, f32[8,2,16,1]{3,2,1,0:T(8,128)} %copy.38.gates_ref, ...), custom_call_target="tpu_custom_call" | custom-call | tf_op jit(solution)/shard_map/pallas_call | solution.py:358
  193.5 2.0 copy.46
  195.4 0.0 copy-start.1
  195.4 3.1 %copy.47 = bf16[1,384,2560]{2,1,0:T(8,128)(2,1)} copy(bf16[1,384,2560]{2,1,0:T(8,128)(2,1)} %bitcast.35) | data formatting | bytes 3932160
  198.5 0.0 copy-done.1
  198.5 0.0 copy-start
  198.5 1.3 copy.48
  199.8 1.0 copy-done
  200.8 1.3 copy.49
  (2 shorter events, 0.0 us)
Async XLA Ops:
  195.4 3.1 %copy-start.1 = (bf16[384,2560]{1,0:T(8,128)(2,1)S(1)}, bf16[384,2560]{1,0:T(8,128)(2,1)}, u32[]{:S(2)}) copy-start(bf16[384,2560]{1,0:T(8,128)(2,1)} %get-tuple-element.10) | copy-start | bytes 5898244
  198.5 2.3 %copy-start = (bf16[384,2560]{1,0:T(8,128)(2,1)S(1)}, bf16[384,2560]{1,0:T(8,128)(2,1)}, u32[]{:S(2)}) copy-start(bf16[384,2560]{1,0:T(8,128)(2,1)} %get-tuple-element.11) | copy-start | bytes 5898244

commit v3 on v2

--- a/solution.py
+++ b/solution.py
@@ -15,12 +15,12 @@
 
 
 def relay_kernel(
-    sections, experts, batches, groups, blk, tile,
+    sections, experts, batches, groups, pair, blk, tile,
     x_ref, cot_ref, gates_ref, place_ref, place_x_ref, place_t_ref, wg_ref, wu_ref, wd_ref,
     out_ref, dwg_ref, dwu_ref, dwd_ref,
-    up_buf, x_send, x_rows, g_send, g_rows, r_send, r_recv, w_other, acts, acts_send, acts_t,
+    up_buf, x_send, x_rows, g_send, g_rows, r_send, r_recv, w_gu, w_d, acts, acts_send, acts_t,
     slope_buf, swish_buf,
-    x_ss, x_rs, g_ss, g_rs, r_ss, r_rs, hop_ss, hop_rs, top_ss, top_rs, w_ss, w_rs,
+    x_ss, x_rs, g_ss, g_rs, r_ss, r_rs, hop_ss, hop_rs, top_ss, top_rs, w_ss, w_rs, w_ls,
     px_ss, px_rs, pg_ss, pg_rs, pa_ss, pa_rs,
 ):
     section = lax.axis_index("section")
@@ -44,6 +44,18 @@
     def peer(step):
         return lax.rem(chip + step, experts)
 
+    own_w = (wg_ref, wu_ref, wd_ref)
+    own_at = [w_gu.at[pl.ds(0, hidden)], w_gu.at[pl.ds(hidden, hidden)], w_d.at[pl.ds(0, hidden)]]
+    other_at = [
+        w_gu.at[pl.ds(2 * hidden, hidden)], w_gu.at[pl.ds(3 * hidden, hidden)],
+        w_d.at[pl.ds(hidden, hidden)],
+    ]
+    local_copies = [
+        pltpu.make_async_copy(own_w[i], own_at[i], w_ls.at[i]) for i in range(3)
+    ]
+    for copy in local_copies:
+        copy.start()
+
     barrier = pltpu.get_barrier_semaphore()
     for step in range(1, experts):
         pl.semaphore_signal(
@@ -103,14 +115,11 @@
             acts_send.at[g], acts.at[1, g], pa_ss.at[g], pa_rs.at[g], section, other
         )
 
-    own_w = (wg_ref, wu_ref, wd_ref)
     weight_copies = [
-        remote(own_w[i], w_other.at[i], w_ss.at[i], w_rs.at[i], section, other) for i in range(3)
+        remote(own_w[i], other_at[i], w_ss.at[i], w_rs.at[i], section, other) for i in range(3)
     ]
 
-    ahead = jnp.where(last, min(2, groups), groups)
-    early = jnp.minimum(1 + 3 * (sections - 1 - section), groups)
-
+    ahead = jnp.where(last, min(pair, groups), groups)
     for copy in weight_copies:
         copy.start()
 
@@ -130,37 +139,34 @@
 
         x_rows[0, g, chip] = x_send[g, chip]
 
-    def weights(which, half):
-        return own_w[which] if half == 0 else w_other.at[which]
-
-    def forward_half(g, half):
-        rows_in = x_rows[0, g].reshape(rows, width)
-        pre_gate = lax.dot_general(
-            rows_in, weights(0, half)[...], COLS, preferred_element_type=F32
-        )
-        pre_up = lax.dot_general(
-            rows_in, weights(1, half)[...], COLS, preferred_element_type=F32
-        )
-        sigmoid = jax.nn.sigmoid(pre_gate)
-        swished = pre_gate * sigmoid
-        columns = pl.ds(half * hidden, hidden)
-        swish_buf[g, :, columns] = swished
-        slope_buf[g, :, columns] = pre_up * (sigmoid * (1.0 + pre_gate * (1.0 - sigmoid)))
-        act = (swished * pre_up).astype(BF16)
-        third = pl.ds(2 * hidden, hidden)
-        if half == 0:
-            acts[0, g, :, third] = act
-        else:
-            acts_send[g, :, third] = act
-
     def rows_arrived(g):
         wait_all(x_send, x_rows.at[0], x_ss, x_rs, g)
         to_partner(x_rows, px_ss, px_rs, g).start()
 
-    def forward(g):
-        rows_arrived(g)
+    def forward(p):
+        first = p * pair
+        for i in range(pair):
+            rows_arrived(first + i)
+        members = pl.ds(first, pair)
+        rows_in = x_rows[0, members].reshape(pair * rows, width)
         for half in range(2):
-            forward_half(g, half)
+            both = lax.dot_general(
+                rows_in, w_gu[pl.ds(half * 2 * hidden, 2 * hidden), :], COLS,
+                preferred_element_type=F32,
+            )
+            pre_gate, pre_up = both[:, :hidden], both[:, hidden:]
+            sigmoid = jax.nn.sigmoid(pre_gate)
+            swished = pre_gate * sigmoid
+            slope = pre_up * (sigmoid * (1.0 + pre_gate * (1.0 - sigmoid)))
+            act = (swished * pre_up).astype(BF16)
+            columns = pl.ds(half * hidden, hidden)
+            swish_buf[members, :, columns] = swished.reshape(pair, rows, hidden)
+            slope_buf[members, :, columns] = slope.reshape(pair, rows, hidden)
+            third = pl.ds(2 * hidden, hidden)
+            if half == 0:
+                acts[0, members, :, third] = act.reshape(pair, rows, hidden)
+            else:
+                acts_send[members, :, third] = act.reshape(pair, rows, hidden)
 
     def dispatch(g):
         @pl.when(last)
@@ -191,32 +197,19 @@
     def backward(g):
         wait_all(g_send, g_rows.at[0], g_ss, g_rs, g)
         rows_grad = g_rows[0, g].reshape(rows, width)
-        slopes = []
-        for half in range(2):
-            d_hidden = lax.dot_general(
-                rows_grad, weights(2, half)[...], COLS, preferred_element_type=F32
-            )
-            columns = pl.ds(half * hidden, hidden)
-            d_gate = (d_hidden * slope_buf[g, :, columns]).astype(BF16)
-            d_up = (d_hidden * swish_buf[g, :, columns]).astype(BF16)
-            slopes.append((d_gate, d_up))
-            if half == 0:
-                acts[0, g, :, pl.ds(0, hidden)] = d_gate
-                acts[0, g, :, pl.ds(hidden, hidden)] = d_up
-            else:
-                acts_send[g, :, pl.ds(0, hidden)] = d_gate
-                acts_send[g, :, pl.ds(hidden, hidden)] = d_up
+        d_hidden = lax.dot_general(rows_grad, w_d[...], COLS, preferred_element_type=F32)
+        d_gate = (d_hidden * slope_buf[g]).astype(BF16)
+        d_up = (d_hidden * swish_buf[g]).astype(BF16)
+        slopes = jnp.concatenate(
+            [d_gate[:, :hidden], d_up[:, :hidden], d_gate[:, hidden:], d_up[:, hidden:]], axis=1
+        )
+        acts[0, g, :, pl.ds(0, 2 * hidden)] = slopes[:, : 2 * hidden]
+        acts_send[g, :, pl.ds(0, 2 * hidden)] = slopes[:, 2 * hidden :]
 
         @pl.loop(0, width // tile)
         def _(t):
             columns = pl.ds(pl.multiple_of(t * tile, 128), tile)
-            total = jnp.zeros((rows, tile), F32)
-            for half in range(2):
-                for which in range(2):
-                    total += jnp.dot(
-                        slopes[half][which], weights(which, half)[:, columns],
-                        preferred_element_type=F32,
-                    )
+            total = jnp.dot(slopes, w_gu[:, columns], preferred_element_type=F32)
             r_send[g, :, :, columns] = total.astype(BF16).reshape(experts, blk, tile)
 
         send_all(r_send, r_recv, r_ss, r_rs, g)
@@ -235,16 +228,15 @@
         def _():
             hop_copy(g).start()
 
-    rows_arrived(0)
-    forward_half(0, 0)
-    weight_copies[0].wait_recv()
-    weight_copies[1].wait_recv()
-    forward_half(0, 1)
-
-    @pl.loop(1, early)
-    def _(g):
-        forward(g)
-
+    for i in range(2):
+        local_copies[i].wait()
+        weight_copies[i].wait_recv()
+
+    @pl.loop(0, jnp.where(last, 0, groups // pair))
+    def _(p):
+        forward(p)
+
+    local_copies[2].wait()
     weight_copies[2].wait_recv()
 
     @pl.loop(0, groups + 1)
@@ -253,13 +245,13 @@
         def _():
             dispatch(g)
 
-        @pl.when(jnp.logical_and(last, g + 2 < groups))
-        def _():
-            send_all(x_send, x_rows.at[0], x_ss, x_rs, g + 2)
-
-        @pl.when(jnp.logical_and(g + 1 >= early, g + 1 < groups))
-        def _():
-            forward(g + 1)
+        @pl.when(jnp.logical_and(last, g + pair < groups))
+        def _():
+            send_all(x_send, x_rows.at[0], x_ss, x_rs, g + pair)
+
+        @pl.when(jnp.logical_and(last, jnp.logical_and(g < groups, lax.rem(g, pair) == 0)))
+        def _():
+            forward(g // pair)
 
         @pl.when(g > 0)
         def _():
@@ -330,6 +322,7 @@
     groups = batches // per
     blk = -(-per * capacity // 16) * 16
     rows = experts * blk
+    pair = 2 if groups % 2 == 0 else 1
     tile = 512 if width % 512 == 0 else 128
 
     flat = routes[0].reshape(batches, tokens * top)
@@ -356,11 +349,11 @@
     dma = pltpu.SemaphoreType.DMA
     grad_w = jax.ShapeDtypeStruct((hidden, width), BF16)
     results = pl.pallas_call(
-        functools.partial(relay_kernel, sections, experts, batches, groups, blk, tile),
+        functools.partial(relay_kernel, sections, experts, batches, groups, pair, blk, tile),
         out_shape=(
             jax.ShapeDtypeStruct((groups, per * tokens, width), BF16), grad_w, grad_w, grad_w,
         ),
-        in_specs=[vmem] * 9,
+        in_specs=[vmem] * 6 + [pl.BlockSpec(memory_space=pl.ANY)] * 3,
         out_specs=(vmem,) * 4,
         scratch_shapes=[
             pltpu.VMEM((groups, per * tokens, width), BF16),
@@ -370,7 +363,8 @@
             pltpu.VMEM((2,) + slots, BF16),
             pltpu.VMEM(slots, BF16),
             pltpu.VMEM(slots, BF16),
-            pltpu.VMEM((3, hidden, width), BF16),
+            pltpu.VMEM((4 * hidden, width), BF16),
+            pltpu.VMEM((2 * hidden, width), BF16),
             pltpu.VMEM((2, groups, rows, 3 * hidden), BF16),
             pltpu.VMEM((groups, rows, 3 * hidden), BF16),
             pltpu.VMEM((3 * hidden, 2 * groups * rows), BF16),
@@ -379,7 +373,7 @@
         ]
         + [dma((groups, experts))] * 6
         + [dma((groups,)), dma((groups,)), dma((groups,)), dma((groups, sections))]
-        + [dma((3,))] * 2
+        + [dma((3,))] * 3
         + [dma((groups,))] * 6,
         compiler_params=pltpu.CompilerParams(
             collective_id=0, has_side_effects=True, vmem_limit_bytes=60 * 2**20

time: 202 us -> 201 us (level)
  no operation moved by 1% of the time
where the time goes in v3:
time: 201 us
  Pallas kernels  186 us (93%)
  local copies, waits for them, and re-layouts  11.9 us (6%)
  other arithmetic  2.29 us (1%)
    pallas_call x1, Pallas kernels, on_device(): pl.pallas_call(functools.partial(relay_kernel, sections, experts, batches...  186 us
    unnamed x10, local copies, waits for them, and re-layouts  10.1 us

profile of v3, /device:TPU:0, one launch (start us, length us, event | category | flops | bytes accessed | tf_op | source)
XLA Modules:
  0.0 200.6 jit_solution(1451733485888700135)
XLA Ops:
  0.6 0.7 copy.41
  1.3 0.8 copy.33
  2.1 0.7 fusion.8
  2.9 0.1 copy.36
  3.0 0.1 copy.35
  3.0 0.1 eq.65
  3.1 0.1 fusion.4
  3.2 0.1 fusion.3
  3.3 0.6 convert_element_type.15.place_t_ref
  4.0 0.8 copy.39.place_x_ref
  4.7 0.8 copy.38.gates_ref
  5.6 0.7 fusion.1.place_ref
  6.3 185.7 %shard_map.102 = (bf16[8,16,2560]{2,1,0:T(8,128)(2,1)}, bf16[384,2560]{1,0:T(8,128)(2,1)}, bf16[384,2560]{1,0:T(8,128)(2,1)}, bf16[384,2560]{1,0:T(8,128)(2,1)}) custom-call(bf16[8,16,2560]{2,1,0:T(8,128)(2,1)} %bitcast.36, bf16[8,16,640]{2,1,0:T(8,128)(2,1)} %cot_ref.1, f32[8,2,16,1]{3,2,1,0:T(8,128)} %copy.38.gates_ref, ...), custom_call_target="tpu_custom_call" | custom-call | tf_op jit(solution)/shard_map/pallas_call | solution.py:351
  192.0 2.0 copy.46
  193.9 0.0 copy-start.1
  193.9 3.1 %copy.47 = bf16[1,384,2560]{2,1,0:T(8,128)(2,1)} copy(bf16[1,384,2560]{2,1,0:T(8,128)(2,1)} %bitcast.35) | data formatting | bytes 3932160
  197.0 0.0 copy-done.1
  197.0 0.0 copy-start
  197.0 1.3 copy.48
  198.3 1.0 copy-done
  199.3 1.3 copy.49
  (2 shorter events, 0.0 us)
Async XLA Ops:
  193.9 3.1 %copy-start.1 = (bf16[384,2560]{1,0:T(8,128)(2,1)S(1)}, bf16[384,2560]{1,0:T(8,128)(2,1)}, u32[]{:S(2)}) copy-start(bf16[384,2560]{1,0:T(8,128)(2,1)} %get-tuple-element.10) | copy-start | bytes 5898244
  197.0 2.3 %copy-start = (bf16[384,2560]{1,0:T(8,128)(2,1)S(1)}, bf16[384,2560]{1,0:T(8,128)(2,1)}, u32[]{:S(2)}) copy-start(bf16[384,2560]{1,0:T(8,128)(2,1)} %get-tuple-element.11) | copy-start | bytes 5898244

commit v4 on v3

--- a/solution.py
+++ b/solution.py
@@ -2,6 +2,7 @@
 
 import jax
 import jax.numpy as jnp
+import numpy as np
 from jax import lax
 from jax.experimental import pallas as pl
 from jax.experimental.pallas import tpu as pltpu
@@ -15,10 +16,10 @@
 
 
 def relay_kernel(
-    sections, experts, batches, groups, pair, blk, tile,
-    x_ref, cot_ref, gates_ref, place_ref, place_x_ref, place_t_ref, wg_ref, wu_ref, wd_ref,
+    sections, experts, batches, groups, pair, fold,
+    x_ref, cot_ref, gates_ref, keys_ref, spots_ref, unpack_ref, pack_ref, wg_ref, wu_ref, wd_ref,
     out_ref, dwg_ref, dwu_ref, dwd_ref,
-    up_buf, x_send, x_rows, g_send, g_rows, r_send, r_recv, w_gu, w_d, acts, acts_send, acts_t,
+    up_buf, x_send, x_wire, x_rows, g_send, g_wire, g_rows, r_send, r_recv, w_gu, w_d, acts, acts_send, acts_t,
     slope_buf, swish_buf,
     x_ss, x_rs, g_ss, g_rs, r_ss, r_rs, hop_ss, hop_rs, top_ss, top_rs, w_ss, w_rs, w_ls,
     px_ss, px_rs, pg_ss, pg_rs, pa_ss, pa_rs,
@@ -29,8 +30,10 @@
     core = place_in % SPLIT
     other = chip * SPLIT + (1 - core)
     last = section == sections - 1
-    rows = experts * blk
+    rows = x_rows.shape[2]
     width = x_ref.shape[2]
+    chunk = width // fold
+    wire = x_send.shape[1:]
     hidden = wg_ref.shape[0]
     piece = cot_ref.shape[2]
     gathered = piece == width
@@ -107,6 +110,33 @@
             jnp.maximum(section - 1, 0), place_in,
         )
 
+    def one_hot(g, k):
+        return jnp.where(spots_ref[...] == keys_ref[g, k], 1.0, 0.0).astype(BF16)
+
+    def both_hot(g):
+        hot = one_hot(g, 0)
+        for k in range(1, keys_ref.shape[1]):
+            hot = hot + one_hot(g, k)
+        return hot
+
+    def stacked(value):
+        return jnp.concatenate(
+            [value[:, c * chunk : (c + 1) * chunk] for c in range(fold)], axis=0
+        )
+
+    def side_by_side(value, count):
+        return jnp.concatenate(
+            [value[c * count : (c + 1) * count] for c in range(fold)], axis=1
+        )
+
+    def unpacked(buf, g):
+        return side_by_side(
+            jnp.dot(
+                unpack_ref[...], buf[g].reshape(fold * rows, chunk), preferred_element_type=F32
+            ).astype(BF16),
+            rows,
+        )
+
     def to_partner(buf, ss, rs, g):
         return remote(buf.at[0, g], buf.at[1, g], ss.at[g], rs.at[g], section, other)
 
@@ -130,17 +160,18 @@
             def _():
                 top_copy(g).start()
 
-        placed = jnp.dot(place_x_ref[g], x_ref[g], preferred_element_type=F32).astype(BF16)
-        x_send[g] = placed.reshape(experts, blk, width)
+        placed = jnp.dot(both_hot(g), stacked(x_ref[g]), preferred_element_type=F32)
+        x_send[g] = placed.astype(BF16).reshape(wire)
 
         @pl.when(g < ahead)
         def _():
-            send_all(x_send, x_rows.at[0], x_ss, x_rs, g)
-
-        x_rows[0, g, chip] = x_send[g, chip]
+            send_all(x_send, x_wire, x_ss, x_rs, g)
+
+        x_wire[g, chip] = x_send[g, chip]
 
     def rows_arrived(g):
-        wait_all(x_send, x_rows.at[0], x_ss, x_rs, g)
+        wait_all(x_send, x_wire, x_ss, x_rs, g)
+        x_rows[0, g] = unpacked(x_wire, g)
         to_partner(x_rows, px_ss, px_rs, g).start()
 
     def forward(p):
@@ -186,17 +217,18 @@
             hop_copy(g).wait_recv()
 
         upstream = up_buf[g].astype(F32)
-        scaled = jnp.concatenate(
-            [(upstream * gates_ref[g, k]).astype(BF16) for k in range(gates_ref.shape[1])], axis=0
-        )
-        placed = jnp.dot(place_ref[g], scaled, preferred_element_type=F32).astype(BF16)
-        g_send[g] = placed.reshape(experts, blk, width)
-        send_all(g_send, g_rows.at[0], g_ss, g_rs, g)
-        g_rows[0, g, chip] = g_send[g, chip]
+        placed = jnp.zeros((fold * rows, chunk), F32)
+        for k in range(gates_ref.shape[1]):
+            scaled = (upstream * gates_ref[g, k]).astype(BF16)
+            placed += jnp.dot(one_hot(g, k), stacked(scaled), preferred_element_type=F32)
+        g_send[g] = placed.astype(BF16).reshape(wire)
+        send_all(g_send, g_wire, g_ss, g_rs, g)
+        g_wire[g, chip] = g_send[g, chip]
 
     def backward(g):
-        wait_all(g_send, g_rows.at[0], g_ss, g_rs, g)
-        rows_grad = g_rows[0, g].reshape(rows, width)
+        wait_all(g_send, g_wire, g_ss, g_rs, g)
+        rows_grad = unpacked(g_wire, g)
+        g_rows[0, g] = rows_grad
         d_hidden = lax.dot_general(rows_grad, w_d[...], COLS, preferred_element_type=F32)
         d_gate = (d_hidden * slope_buf[g]).astype(BF16)
         d_up = (d_hidden * swish_buf[g]).astype(BF16)
@@ -206,12 +238,18 @@
         acts[0, g, :, pl.ds(0, 2 * hidden)] = slopes[:, : 2 * hidden]
         acts_send[g, :, pl.ds(0, 2 * hidden)] = slopes[:, 2 * hidden :]
 
-        @pl.loop(0, width // tile)
-        def _(t):
-            columns = pl.ds(pl.multiple_of(t * tile, 128), tile)
-            total = jnp.dot(slopes, w_gu[:, columns], preferred_element_type=F32)
-            r_send[g, :, :, columns] = total.astype(BF16).reshape(experts, blk, tile)
-
+        half = width // 2
+        total = jnp.concatenate(
+            [
+                jnp.dot(
+                    slopes, w_gu[:, pl.ds(i * half, half)], preferred_element_type=F32
+                ).astype(BF16)
+                for i in range(2)
+            ],
+            axis=1,
+        )
+        packed = jnp.dot(pack_ref[...], stacked(total), preferred_element_type=F32)
+        r_send[g] = packed.astype(BF16).reshape(wire)
         send_all(r_send, r_recv, r_ss, r_rs, g)
         r_recv[g, chip] = r_send[g, chip]
         to_partner(g_rows, pg_ss, pg_rs, g).start()
@@ -219,9 +257,11 @@
 
     def combine(g):
         wait_all(r_send, r_recv, r_ss, r_rs, g)
-        back = jnp.dot(
-            place_t_ref[g], r_recv[g].reshape(rows, width), preferred_element_type=F32
-        )
+        picked = lax.dot_general(
+            both_hot(g), r_recv[g].reshape(fold * rows, chunk), (((0,), (0,)), ((), ())),
+            preferred_element_type=F32,
+        )
+        back = side_by_side(picked, x_ref.shape[1])
         out_ref[g] = (up_buf[g].astype(F32) + back).astype(BF16)
 
         @pl.when(section > 0)
@@ -247,7 +287,7 @@
 
         @pl.when(jnp.logical_and(last, g + pair < groups))
         def _():
-            send_all(x_send, x_rows.at[0], x_ss, x_rs, g + pair)
+            send_all(x_send, x_wire, x_ss, x_rs, g + pair)
 
         @pl.when(jnp.logical_and(last, jnp.logical_and(g < groups, lax.rem(g, pair) == 0)))
         def _():
@@ -277,8 +317,8 @@
     @pl.loop(0, width // 256)
     def _(t):
         columns = pl.ds(pl.multiple_of(t * 256, 128), 256)
-        rows_in = x_rows[:, :, :, :, columns].reshape(total_rows, 256)
-        rows_grad = g_rows[:, :, :, :, columns].reshape(total_rows, 256)
+        rows_in = x_rows[:, :, :, columns].reshape(total_rows, 256)
+        rows_grad = g_rows[:, :, :, columns].reshape(total_rows, 256)
         for i, (result, side) in enumerate(
             ((dwg_ref, rows_in), (dwu_ref, rows_in), (dwd_ref, rows_grad))
         ):
@@ -289,8 +329,8 @@
 
     @pl.loop(0, groups)
     def _(g):
-        wait_sent(x_send, x_rows.at[0], x_ss, x_rs, g)
-        wait_sent(g_send, g_rows.at[0], g_ss, g_rs, g)
+        wait_sent(x_send, x_wire, x_ss, x_rs, g)
+        wait_sent(g_send, g_wire, g_ss, g_rs, g)
         wait_sent(r_send, r_recv, r_ss, r_rs, g)
         to_partner(x_rows, px_ss, px_rs, g).wait_send()
         to_partner(g_rows, pg_ss, pg_rs, g).wait_send()
@@ -320,22 +360,30 @@
     while per * capacity < group_rows and batches % (2 * per) == 0:
         per *= 2
     groups = batches // per
-    blk = -(-per * capacity // 16) * 16
-    rows = experts * blk
+    block = per * capacity
+    fold = 0
+    for parts in (4, 2, 1):
+        if block * parts % 16 == 0 and experts * block % 16 == 0 and width % (128 * parts) == 0:
+            fold = parts
+    if fold == 0:
+        fold, block = 1, -(-block // 16) * 16
+    rows = experts * block
     pair = 2 if groups % 2 == 0 else 1
-    tile = 512 if width % 512 == 0 else 128
 
     flat = routes[0].reshape(batches, tokens * top)
     hot = (flat[:, :, None] == jnp.arange(experts, dtype=jnp.int32)).astype(jnp.int32)
     earlier = jnp.cumsum(hot, axis=1) - hot
     within = jnp.sum(earlier * hot, axis=2)
     batch_in = jnp.arange(batches, dtype=jnp.int32)[:, None] % per
-    target = (flat * blk + batch_in * capacity + within).reshape(groups, per, tokens, top)
-    target = jnp.transpose(target, (0, 3, 1, 2)).reshape(groups, top, per * tokens)
-    spots = jnp.arange(rows, dtype=jnp.int32)
-    place = (spots[None, :, None] == target.reshape(groups, 1, -1)).astype(BF16)
-    place_x = jnp.any(spots[None, :, None, None] == target[:, None], axis=2).astype(BF16)
-    place_t = jnp.any(target[:, :, :, None] == spots, axis=1).astype(BF16)
+    target = (flat * block + batch_in * capacity + within).reshape(groups, per, tokens, top)
+    target = jnp.transpose(target, (0, 3, 1, 2)).reshape(groups, top, 1, per * tokens)
+    chunks = jnp.arange(fold, dtype=jnp.int32)[:, None] * rows
+    keys = (target + chunks).reshape(groups, top, 1, fold * per * tokens)
+    on_wire = np.transpose(
+        np.arange(fold * rows, dtype=np.int32).reshape(fold, experts, block), (1, 0, 2)
+    ).reshape(-1)
+    spots = np.repeat(on_wire[:, None], fold * per * tokens, axis=1)
+    pack = (on_wire[:, None] == np.arange(fold * rows)[None, :]).astype(np.float32)
     scales = jnp.transpose(
         gates[0].reshape(groups, per * tokens, top), (0, 2, 1)
     )[..., None]
@@ -345,22 +393,25 @@
     cot_groups = cotangent.reshape(groups, per * tokens, cotangent.shape[2])
 
     vmem = pl.BlockSpec(memory_space=pltpu.VMEM)
-    slots = (groups, experts, blk, width)
+    slots = (groups, experts, fold * block, width // fold)
+    whole = (2, groups, rows, width)
     dma = pltpu.SemaphoreType.DMA
     grad_w = jax.ShapeDtypeStruct((hidden, width), BF16)
     results = pl.pallas_call(
-        functools.partial(relay_kernel, sections, experts, batches, groups, pair, blk, tile),
+        functools.partial(relay_kernel, sections, experts, batches, groups, pair, fold),
         out_shape=(
             jax.ShapeDtypeStruct((groups, per * tokens, width), BF16), grad_w, grad_w, grad_w,
         ),
-        in_specs=[vmem] * 6 + [pl.BlockSpec(memory_space=pl.ANY)] * 3,
+        in_specs=[vmem] * 7 + [pl.BlockSpec(memory_space=pl.ANY)] * 3,
         out_specs=(vmem,) * 4,
         scratch_shapes=[
             pltpu.VMEM((groups, per * tokens, width), BF16),
             pltpu.VMEM(slots, BF16),
-            pltpu.VMEM((2,) + slots, BF16),
-            pltpu.VMEM(slots, BF16),
-            pltpu.VMEM((2,) + slots, BF16),
+            pltpu.VMEM(slots, BF16),
+            pltpu.VMEM(whole, BF16),
+            pltpu.VMEM(slots, BF16),
+            pltpu.VMEM(slots, BF16),
+            pltpu.VMEM(whole, BF16),
             pltpu.VMEM(slots, BF16),
             pltpu.VMEM(slots, BF16),
             pltpu.VMEM((4 * hidden, width), BF16),
@@ -379,7 +430,8 @@
             collective_id=0, has_side_effects=True, vmem_limit_bytes=60 * 2**20
         ),
     )(
-        x_groups, cot_groups, scales, place, place_x, place_t, w_gate[0], w_up[0], w_down[0]
+        x_groups, cot_groups, scales, keys, jnp.asarray(spots),
+        jnp.asarray(pack.T, BF16), jnp.asarray(pack, BF16), w_gate[0], w_up[0], w_down[0]
     )
     grad_inputs = results[0].reshape(1, batches, tokens, width)
     return (grad_inputs, results[1][None], results[2][None], results[3][None])

time: 201 us -> 179 us (0.89)
  Pallas kernels: 186 us -> 165 us
    pallas_call x1, Pallas kernels: 186 us -> 165 us  [on_device(): pl.pallas_call(functools.partial(relay_kernel, sections, experts, batches...]
where the time goes in v4:
time: 179 us; the launch traced here: 178 us
  Pallas kernels  165 us (92%)
  local copies, waits for them, and re-layouts  11.2 us (6%)
    pallas_call x1, Pallas kernels, on_device(): pl.pallas_call(functools.partial(relay_kernel, sections, experts, batches...  165 us
    unnamed x10, local copies, waits for them, and re-layouts  10.1 us

profile of v4, /device:TPU:0, one launch (start us, length us, event | category | flops | bytes accessed | tf_op | source)
XLA Modules:
  0.0 178.2 jit_solution(9901141648557227374)
XLA Ops:
  0.6 0.1 add.51
  0.7 0.1 add.52
  0.8 0.7 copy.20
  1.5 0.8 copy.15
  2.3 0.7 fusion.4
  3.0 0.1 copy.17
  3.1 0.1 add.50
  3.2 0.6 broadcast_add_fusion.keys_ref
  3.8 0.8 copy.18.gates_ref
  4.7 165.0 %shard_map.129 = (bf16[8,16,2560]{2,1,0:T(8,128)(2,1)}, bf16[384,2560]{1,0:T(8,128)(2,1)}, bf16[384,2560]{1,0:T(8,128)(2,1)}, bf16[384,2560]{1,0:T(8,128)(2,1)}) custom-call(bf16[8,16,2560]{2,1,0:T(8,128)(2,1)} %bitcast.32, bf16[8,16,640]{2,1,0:T(8,128)(2,1)} %cot_ref.1, f32[8,2,16,1]{3,2,1,0:T(8,128)} %copy.18.gates_ref, ...), custom_call_target="tpu_custom_call" | custom-call | tf_op jit(solution)/shard_map/pallas_call | solution.py:400
  169.7 2.0 %copy.25 = bf16[1,8,16,2560]{3,2,1,0:T(8,128)(2,1)} copy(bf16[1,8,16,2560]{3,2,1,0:T(8,128)(2,1)} %bitcast.31) | data formatting | bytes 1310720
  171.6 0.0 copy-start.1
  171.6 3.1 %copy.26 = bf16[1,384,2560]{2,1,0:T(8,128)(2,1)} copy(bf16[1,384,2560]{2,1,0:T(8,128)(2,1)} %bitcast.27) | data formatting | bytes 3932160
  174.7 0.0 copy-done.1
  174.7 0.0 copy-start
  174.7 1.3 copy.27
  176.0 1.0 copy-done
  177.0 1.3 copy.28
  (3 shorter events, 0.0 us)
Async XLA Ops:
  171.6 3.1 %copy-start.1 = (bf16[384,2560]{1,0:T(8,128)(2,1)S(1)}, bf16[384,2560]{1,0:T(8,128)(2,1)}, u32[]{:S(2)}) copy-start(bf16[384,2560]{1,0:T(8,128)(2,1)} %get-tuple-element.10) | copy-start | bytes 5898244
  174.7 2.3 %copy-start = (bf16[384,2560]{1,0:T(8,128)(2,1)S(1)}, bf16[384,2560]{1,0:T(8,128)(2,1)}, u32[]{:S(2)}) copy-start(bf16[384,2560]{1,0:T(8,128)(2,1)} %get-tuple-element.11) | copy-start | bytes 5898244

commit v5 on v4

--- a/solution.py
+++ b/solution.py
@@ -153,21 +153,22 @@
     for copy in weight_copies:
         copy.start()
 
-    @pl.loop(0, groups)
-    def _(g):
-        if not gathered:
-            @pl.when(jnp.logical_not(last))
-            def _():
-                top_copy(g).start()
-
+    def place_inputs(g):
         placed = jnp.dot(both_hot(g), stacked(x_ref[g]), preferred_element_type=F32)
         x_send[g] = placed.astype(BF16).reshape(wire)
-
-        @pl.when(g < ahead)
-        def _():
-            send_all(x_send, x_wire, x_ss, x_rs, g)
-
         x_wire[g, chip] = x_send[g, chip]
+
+    if not gathered:
+        @pl.when(jnp.logical_not(last))
+        def _():
+            @pl.loop(0, groups)
+            def _(g):
+                top_copy(g).start()
+
+    @pl.loop(0, ahead)
+    def _(g):
+        place_inputs(g)
+        send_all(x_send, x_wire, x_ss, x_rs, g)
 
     def rows_arrived(g):
         wait_all(x_send, x_wire, x_ss, x_rs, g)
@@ -227,6 +228,11 @@
 
     def backward(g):
         wait_all(g_send, g_wire, g_ss, g_rs, g)
+
+        @pl.when(jnp.logical_and(last, g + pair < groups))
+        def _():
+            send_all(x_send, x_wire, x_ss, x_rs, g + pair)
+
         rows_grad = unpacked(g_wire, g)
         g_rows[0, g] = rows_grad
         d_hidden = lax.dot_general(rows_grad, w_d[...], COLS, preferred_element_type=F32)
@@ -268,16 +274,21 @@
         def _():
             hop_copy(g).start()
 
-    for i in range(2):
-        local_copies[i].wait()
-        weight_copies[i].wait_recv()
-
-    @pl.loop(0, jnp.where(last, 0, groups // pair))
-    def _(p):
-        forward(p)
-
-    local_copies[2].wait()
-    weight_copies[2].wait_recv()
+    def wait_weights(first, end):
+        for i in range(first, end):
+            local_copies[i].wait()
+            weight_copies[i].wait_recv()
+
+    pairs = groups // pair
+    upfront = jnp.minimum(2 * (sections - 1 - section), pairs)
+
+    @pl.when(jnp.logical_not(last))
+    def _():
+        wait_weights(0, 2)
+
+        @pl.loop(0, upfront)
+        def _(p):
+            forward(p)
 
     @pl.loop(0, groups + 1)
     def _(g):
@@ -287,11 +298,19 @@
 
         @pl.when(jnp.logical_and(last, g + pair < groups))
         def _():
-            send_all(x_send, x_wire, x_ss, x_rs, g + pair)
-
-        @pl.when(jnp.logical_and(last, jnp.logical_and(g < groups, lax.rem(g, pair) == 0)))
-        def _():
-            forward(g // pair)
+            place_inputs(g + pair)
+
+        @pl.when(jnp.logical_and(last, g == 0))
+        def _():
+            wait_weights(0, 2)
+
+        @pl.when(jnp.logical_and(g // pair + upfront < pairs, lax.rem(g, pair) == 0))
+        def _():
+            forward(g // pair + upfront)
+
+        @pl.when(g == 0)
+        def _():
+            wait_weights(2, 3)
 
         @pl.when(g > 0)
         def _():

time: 179 us -> 176 us (0.983)
  Pallas kernels: 165 us -> 163 us
    pallas_call x1, Pallas kernels: 165 us -> 163 us  [on_device(): pl.pallas_call(functools.partial(relay_kernel, sections, experts, batches...]
where the time goes in v5:
time: 176 us
  Pallas kernels  163 us (93%)
  local copies, waits for them, and re-layouts  11.2 us (6%)
    pallas_call x1, Pallas kernels, on_device(): pl.pallas_call(functools.partial(relay_kernel, sections, experts, batches...  163 us
    unnamed x10, local copies, waits for them, and re-layouts  10.1 us

profile of v5, /device:TPU:0, one launch (start us, length us, event | category | flops | bytes accessed | tf_op | source)
XLA Modules:
  0.0 176.0 jit_solution(14729053829880924556)
XLA Ops:
  0.6 0.1 add.51
  0.7 0.1 add.52
  0.8 0.7 copy.20
  1.5 0.8 copy.15
  2.3 0.7 fusion.4
  3.0 0.1 copy.17
  3.1 0.1 add.50
  3.2 0.6 broadcast_add_fusion.keys_ref
  3.8 0.8 copy.18.gates_ref
  4.7 162.7 %shard_map.129 = (bf16[8,16,2560]{2,1,0:T(8,128)(2,1)}, bf16[384,2560]{1,0:T(8,128)(2,1)}, bf16[384,2560]{1,0:T(8,128)(2,1)}, bf16[384,2560]{1,0:T(8,128)(2,1)}) custom-call(bf16[8,16,2560]{2,1,0:T(8,128)(2,1)} %bitcast.32, bf16[8,16,640]{2,1,0:T(8,128)(2,1)} %cot_ref.1, f32[8,2,16,1]{3,2,1,0:T(8,128)} %copy.18.gates_ref, ...), custom_call_target="tpu_custom_call" | custom-call | tf_op jit(solution)/shard_map/pallas_call | solution.py:419
  167.4 2.0 %copy.25 = bf16[1,8,16,2560]{3,2,1,0:T(8,128)(2,1)} copy(bf16[1,8,16,2560]{3,2,1,0:T(8,128)(2,1)} %bitcast.31) | data formatting | bytes 1310720
  169.3 0.0 copy-start.1
  169.3 3.1 %copy.26 = bf16[1,384,2560]{2,1,0:T(8,128)(2,1)} copy(bf16[1,384,2560]{2,1,0:T(8,128)(2,1)} %bitcast.27) | data formatting | bytes 3932160
  172.4 0.0 copy-done.1
  172.4 0.0 copy-start
  172.4 1.3 copy.27
  173.7 1.0 copy-done
  174.7 1.3 copy.28
  (3 shorter events, 0.0 us)
Async XLA Ops:
  169.3 3.1 %copy-start.1 = (bf16[384,2560]{1,0:T(8,128)(2,1)S(1)}, bf16[384,2560]{1,0:T(8,128)(2,1)}, u32[]{:S(2)}) copy-start(bf16[384,2560]{1,0:T(8,128)(2,1)} %get-tuple-element.10) | copy-start | bytes 5898244
  172.4 2.3 %copy-start = (bf16[384,2560]{1,0:T(8,128)(2,1)S(1)}, bf16[384,2560]{1,0:T(8,128)(2,1)}, u32[]{:S(2)}) copy-start(bf16[384,2560]{1,0:T(8,128)(2,1)} %get-tuple-element.11) | copy-start | bytes 5898244

commit v6 on v5

--- a/solution.py
+++ b/solution.py
@@ -10,7 +10,6 @@
 
 SPLIT = 2
 MESH = pl.DeviceIdType.MESH
-COLS = (((1,), (1,)), ((), ()))
 F32 = jnp.float32
 BF16 = jnp.bfloat16
 
@@ -19,7 +18,7 @@
     sections, experts, batches, groups, pair, fold,
     x_ref, cot_ref, gates_ref, keys_ref, spots_ref, unpack_ref, pack_ref, wg_ref, wu_ref, wd_ref,
     out_ref, dwg_ref, dwu_ref, dwd_ref,
-    up_buf, x_send, x_wire, x_rows, g_send, g_wire, g_rows, r_send, r_recv, w_gu, w_d, acts, acts_send, acts_t,
+    up_buf, x_send, x_wire, x_rows, g_send, g_wire, g_rows, r_send, r_recv, w_gu, w_d, w_gut, w_dt, acts, acts_send, acts_t,
     slope_buf, swish_buf,
     x_ss, x_rs, g_ss, g_rs, r_ss, r_rs, hop_ss, hop_rs, top_ss, top_rs, w_ss, w_rs, w_ls,
     px_ss, px_rs, pg_ss, pg_rs, pa_ss, pa_rs,
@@ -182,8 +181,8 @@
         members = pl.ds(first, pair)
         rows_in = x_rows[0, members].reshape(pair * rows, width)
         for half in range(2):
-            both = lax.dot_general(
-                rows_in, w_gu[pl.ds(half * 2 * hidden, 2 * hidden), :], COLS,
+            both = jnp.dot(
+                rows_in, w_gut[:, pl.ds(half * 2 * hidden, 2 * hidden)],
                 preferred_element_type=F32,
             )
             pre_gate, pre_up = both[:, :hidden], both[:, hidden:]
@@ -235,7 +234,7 @@
 
         rows_grad = unpacked(g_wire, g)
         g_rows[0, g] = rows_grad
-        d_hidden = lax.dot_general(rows_grad, w_d[...], COLS, preferred_element_type=F32)
+        d_hidden = jnp.dot(rows_grad, w_dt[...], preferred_element_type=F32)
         d_gate = (d_hidden * slope_buf[g]).astype(BF16)
         d_up = (d_hidden * swish_buf[g]).astype(BF16)
         slopes = jnp.concatenate(
@@ -274,13 +273,28 @@
         def _():
             hop_copy(g).start()
 
+    def turn(source, result, first, count):
+        @pl.loop(0, width // 256)
+        def _(t):
+            span = pl.ds(pl.multiple_of(t * 256, 256), 256)
+            result[span, pl.ds(first, count)] = source[pl.ds(first, count), span].T
+
     def wait_weights(first, end):
         for i in range(first, end):
             local_copies[i].wait()
+        if first == 0:
+            turn(w_gu, w_gut, 0, 2 * hidden)
+        else:
+            turn(w_d, w_dt, 0, hidden)
+        for i in range(first, end):
             weight_copies[i].wait_recv()
+        if first == 0:
+            turn(w_gu, w_gut, 2 * hidden, 2 * hidden)
+        else:
+            turn(w_d, w_dt, hidden, hidden)
 
     pairs = groups // pair
-    upfront = jnp.minimum(2 * (sections - 1 - section), pairs)
+    upfront = jnp.where(last, 0, jnp.minimum(sections - section, pairs))
 
     @pl.when(jnp.logical_not(last))
     def _():
@@ -387,7 +401,7 @@
     if fold == 0:
         fold, block = 1, -(-block // 16) * 16
     rows = experts * block
-    pair = 2 if groups % 2 == 0 else 1
+    pair = 2 if groups % 2 == 0 and rows <= 128 else 1
 
     flat = routes[0].reshape(batches, tokens * top)
     hot = (flat[:, :, None] == jnp.arange(experts, dtype=jnp.int32)).astype(jnp.int32)
@@ -435,6 +449,8 @@
             pltpu.VMEM(slots, BF16),
             pltpu.VMEM((4 * hidden, width), BF16),
             pltpu.VMEM((2 * hidden, width), BF16),
+            pltpu.VMEM((width, 4 * hidden), BF16),
+            pltpu.VMEM((width, 2 * hidden), BF16),
             pltpu.VMEM((2, groups, rows, 3 * hidden), BF16),
             pltpu.VMEM((groups, rows, 3 * hidden), BF16),
             pltpu.VMEM((3 * hidden, 2 * groups * rows), BF16),
@@ -446,7 +462,7 @@
         + [dma((3,))] * 3
         + [dma((groups,))] * 6,
         compiler_params=pltpu.CompilerParams(
-            collective_id=0, has_side_effects=True, vmem_limit_bytes=60 * 2**20
+            collective_id=0, has_side_effects=True, vmem_limit_bytes=62 * 2**20
         ),
     )(
         x_groups, cot_groups, scales, keys, jnp.asarray(spots),

time: 176 us -> 171 us (0.972)
  Pallas kernels: 163 us -> 158 us
    pallas_call x1, Pallas kernels: 163 us -> 158 us  [on_device(): pl.pallas_call(functools.partial(relay_kernel, sections, experts, batches...]
where the time goes in v6:
time: 171 us
  Pallas kernels  158 us (92%)
  local copies, waits for them, and re-layouts  11.2 us (7%)
    pallas_call x1, Pallas kernels, on_device(): pl.pallas_call(functools.partial(relay_kernel, sections, experts, batches...  158 us
    unnamed x10, local copies, waits for them, and re-layouts  10.1 us

profile of v6, /device:TPU:0, one launch (start us, length us, event | category | flops | bytes accessed | tf_op | source)
XLA Modules:
  0.0 171.0 jit_solution(5511197444654288207)
XLA Ops:
  0.6 0.1 add.51
  0.7 0.1 add.52
  0.8 0.7 copy.20
  1.5 0.8 copy.15
  2.3 0.7 fusion.4
  3.0 0.1 copy.17
  3.1 0.1 add.50
  3.2 0.6 broadcast_add_fusion.keys_ref
  3.8 0.8 copy.18.gates_ref
  4.7 157.8 %shard_map.129 = (bf16[8,16,2560]{2,1,0:T(8,128)(2,1)}, bf16[384,2560]{1,0:T(8,128)(2,1)}, bf16[384,2560]{1,0:T(8,128)(2,1)}, bf16[384,2560]{1,0:T(8,128)(2,1)}) custom-call(bf16[8,16,2560]{2,1,0:T(8,128)(2,1)} %bitcast.32, bf16[8,16,640]{2,1,0:T(8,128)(2,1)} %cot_ref.1, f32[8,2,16,1]{3,2,1,0:T(8,128)} %copy.18.gates_ref, ...), custom_call_target="tpu_custom_call" | custom-call | tf_op jit(solution)/shard_map/pallas_call | solution.py:433
  162.5 2.0 %copy.25 = bf16[1,8,16,2560]{3,2,1,0:T(8,128)(2,1)} copy(bf16[1,8,16,2560]{3,2,1,0:T(8,128)(2,1)} %bitcast.31) | data formatting | bytes 1310720
  164.4 0.0 copy-start.1
  164.4 3.1 %copy.26 = bf16[1,384,2560]{2,1,0:T(8,128)(2,1)} copy(bf16[1,384,2560]{2,1,0:T(8,128)(2,1)} %bitcast.27) | data formatting | bytes 3932160
  167.5 0.0 copy-done.1
  167.5 0.0 copy-start
  167.5 1.3 copy.27
  168.8 1.0 copy-done
  169.8 1.3 copy.28
  (3 shorter events, 0.0 us)
Async XLA Ops:
  164.4 3.1 %copy-start.1 = (bf16[384,2560]{1,0:T(8,128)(2,1)S(1)}, bf16[384,2560]{1,0:T(8,128)(2,1)}, u32[]{:S(2)}) copy-start(bf16[384,2560]{1,0:T(8,128)(2,1)} %get-tuple-element.10) | copy-start | bytes 5898244
  167.5 2.3 %copy-start = (bf16[384,2560]{1,0:T(8,128)(2,1)S(1)}, bf16[384,2560]{1,0:T(8,128)(2,1)}, u32[]{:S(2)}) copy-start(bf16[384,2560]{1,0:T(8,128)(2,1)} %get-tuple-element.11) | copy-start | bytes 5898244
